TPU v7x, 32 devices: a whole 2x2x4 slice. The times are simulated.
32 devices in a mesh: dp: 2 (over core), pipe: 4 (over y, x), ctx: 4 (over z).
Axes of the slice: x: 2, y: 2, z: 4, core: 2. Of those that a mesh axis runs over, the one named last changes fastest.
Arguments:
- inputs: bfloat16 [4, 256, 768], P('dp', 'ctx'), may hold values from -6 to 6
- cotangent: bfloat16 [4, 256, 768], P('dp', 'ctx'), may hold values from -6 to 6
- dilated_kernel_weight: bfloat16 [4, 3, 768, 384], P('pipe'), may hold values from -0.125 to 0.125
- point_weight: bfloat16 [4, 384, 768], P('pipe'), may hold values from -0.3125 to 0.3125
Outputs:
- dilated_grad: float32 [4, 3, 768, 384], P('pipe', None, ('dp', 'ctx'))
All inputs are finite; a program needn't handle non-finite values.
Results may differ from a plain program's by a relative error of at most 0.012.
Values may be sent and summed in bfloat16 or wider, within the bound.
No kernel may reach another device: no remote copies, remote signals or barrier semaphores. Data moves between devices by JAX's collectives and lax.ppermute only.
A program may use at most 64 MiB of HBM per device.

v0:
```python
import functools
import math

import jax
import jax.numpy as jnp
from jax import lax
from jax.experimental import pallas as pl
from jax.experimental.pallas import tpu as pltpu
from jax.sharding import PartitionSpec as P

root_half = 0.7071067811865476
inv_root_two_pi = 0.3989422804014327

in_vmem = pl.BlockSpec(memory_space=pltpu.VMEM)
anywhere = pl.BlockSpec(memory_space=pl.ANY)
contract_last = (((1,), (1,)), ((), ()))
contract_first = (((0,), (0,)), ((), ()))


def gelu(value):
    return 0.5 * value * (1.0 + lax.erf(value * root_half))


def gelu_slope(value):
    return (
        0.5 * (1.0 + lax.erf(value * root_half))
        + value * jnp.exp(-0.5 * value * value) * inv_root_two_pi
    )


def padded(cells, sides, width):
    for axis, dim in sides:
        count = lax.axis_size(axis)
        ends = count - 1
        head = lax.slice_in_dim(cells, 0, width, axis=dim)
        tail = lax.slice_in_dim(cells, cells.shape[dim] - width, cells.shape[dim], axis=dim)
        cells = jnp.concatenate(
            [
                lax.ppermute(tail, axis, [(i, (i + 1) % count) for i in range(ends)]),
                cells,
                lax.ppermute(head, axis, [((i + 1) % count, i) for i in range(ends)]),
            ],
            axis=dim,
        )
    return cells


def shifted(block, axis, distance):
    devices = range(lax.axis_size(axis))
    route = [(i - distance, i) for i in devices if i - distance in devices]
    return lax.ppermute(block, axis, route)


def edge_shards(inputs, cotangent, dilated_kernel_weight, point_weight):
    sections = lax.axis_size("pipe")
    section = lax.axis_index("pipe")
    seq_count, bins, chans = inputs.shape
    reach = bins // 2
    table = jnp.array(
        [reach // 2 ** (sections - 1 - level) for level in range(sections)], jnp.int32
    )
    spread = table[section]
    dilation_weight = dilated_kernel_weight[0]
    w_point = point_weight[0]
    inner_channel_count = dilation_weight.shape[2]
    scale = 1.0 / math.sqrt(seq_count * lax.axis_size("dp") * bins * lax.axis_size("ctx"))
    ticks = jnp.arange(seq_count + sections - 1, dtype=jnp.int32)

    def conv_fore(extended):
        running_total = jnp.zeros((bins, inner_channel_count), jnp.float32)
        for kernel_offset in range(3):
            receptive_span = lax.dynamic_slice_in_dim(
                extended, reach + (kernel_offset - 1) * spread, bins, 0
            )
            running_total = running_total + jnp.dot(
                receptive_span, dilation_weight[kernel_offset], preferred_element_type=jnp.float32
            )
        return running_total

    def put(store, slot, valid, item):
        current = lax.dynamic_index_in_dim(store, slot, 0, keepdims=False)
        return lax.dynamic_update_index_in_dim(store, jnp.where(valid, item, current), slot, 0)

    kept_x = jnp.zeros(inputs.shape, jnp.bfloat16)
    kept_ext = jnp.zeros((seq_count, bins + 2 * reach, chans), jnp.bfloat16)
    kept_pre = jnp.zeros((seq_count, bins, inner_channel_count), jnp.float32)

    def fore_tick(carry, tick):
        received, store_x, store_ext, store_pre = carry
        micro = tick - section
        valid = (micro >= 0) & (micro < seq_count)
        slot = jnp.clip(micro, 0, seq_count - 1)
        first = lax.dynamic_index_in_dim(inputs, slot, 0, keepdims=False)
        trunk_in = jnp.where(section == 0, first, received)
        act = gelu(trunk_in.astype(jnp.float32)).astype(jnp.bfloat16)
        extended = padded(act, (("ctx", 0),), reach)
        pre = conv_fore(extended)
        inner = gelu(pre).astype(jnp.bfloat16)
        out = (
            trunk_in.astype(jnp.float32)
            + jnp.dot(inner, w_point, preferred_element_type=jnp.float32)
        ).astype(jnp.bfloat16)
        sent = shifted(out, "pipe", 1)
        store_x = put(store_x, slot, valid, trunk_in)
        store_ext = put(store_ext, slot, valid, extended)
        store_pre = put(store_pre, slot, valid, pre)
        return ((sent, store_x, store_ext, store_pre), None)

    start_recv = jnp.zeros((bins, chans), jnp.bfloat16)
    (unused, kept_x, kept_ext, kept_pre), unused_out = lax.scan(
        fore_tick, (start_recv, kept_x, kept_ext, kept_pre), ticks
    )

    def back_tick(carry, tick):
        received, grad = carry
        micro = tick - (sections - 1 - section)
        valid = (micro >= 0) & (micro < seq_count)
        slot = jnp.clip(micro, 0, seq_count - 1)
        last = (
            lax.dynamic_index_in_dim(cotangent, slot, 0, keepdims=False).astype(jnp.float32) * scale
        ).astype(jnp.bfloat16)
        upstream = jnp.where(section == sections - 1, last, received)
        trunk_in = lax.dynamic_index_in_dim(kept_x, slot, 0, keepdims=False)
        extended = lax.dynamic_index_in_dim(kept_ext, slot, 0, keepdims=False)
        pre = lax.dynamic_index_in_dim(kept_pre, slot, 0, keepdims=False)
        inner_grad = lax.dot_general(
            upstream, w_point, contract_last, preferred_element_type=jnp.float32
        )
        dpre = (inner_grad * gelu_slope(pre) * valid.astype(jnp.float32)).astype(jnp.bfloat16)
        dpre_ext = padded(dpre, (("ctx", 0),), reach)
        dact = jnp.zeros((bins, chans), jnp.float32)
        taps = []
        for kernel_offset in range(3):
            receptive_span = lax.dynamic_slice_in_dim(
                dpre_ext, reach - (kernel_offset - 1) * spread, bins, 0
            )
            dact = dact + lax.dot_general(
                receptive_span,
                dilation_weight[kernel_offset],
                contract_last,
                preferred_element_type=jnp.float32,
            )
            source = lax.dynamic_slice_in_dim(
                extended, reach + (kernel_offset - 1) * spread, bins, 0
            )
            taps.append(
                lax.dot_general(source, dpre, contract_first, preferred_element_type=jnp.float32)
            )
        grad = grad + jnp.stack(taps)
        back = (
            upstream.astype(jnp.float32) + dact * gelu_slope(trunk_in.astype(jnp.float32))
        ).astype(jnp.bfloat16)
        sent = shifted(back, "pipe", -1)
        return ((sent, grad), None)

    start_grad = jnp.zeros((3, chans, inner_channel_count), jnp.float32)
    (unused_back, grad), unused_seq = lax.scan(back_tick, (start_recv, start_grad), ticks)
    term = grad[None]
    return lax.psum_scatter(term, ("dp", "ctx"), scatter_dimension=2, tiled=True)


def moved(value, by, bins):
    pieces = []
    for start in range(0, value.shape[0], bins):
        piece = value[start : start + bins]
        place = lax.broadcasted_iota(jnp.int32, piece.shape, 0)
        if by > 0:
            keep = place >= by
        else:
            keep = place < bins + by
        pieces.append(jnp.where(keep, pltpu.roll(piece, by % bins, 0), 0.0))
    return jnp.concatenate(pieces, axis=0)


def fore(x, weight_ref, spread, bins):
    act = gelu(x.astype(jnp.float32)).astype(jnp.bfloat16)
    terms = [
        jnp.dot(act, weight_ref[0, tap], preferred_element_type=jnp.float32) for tap in range(3)
    ]
    return terms[1] + moved(terms[0], spread, bins) + moved(terms[2], -spread, bins)


def back_pre(dy, pre_slope, point_ref):
    inner_grad = jnp.dot(dy, point_ref[0], preferred_element_type=jnp.float32)
    return (inner_grad * pre_slope).astype(jnp.bfloat16)


def back_trunk(dy, dpre, x_slope, weight_ref, spread, bins):
    wide = dpre.astype(jnp.float32)
    spans = (
        moved(wide, -spread, bins).astype(jnp.bfloat16),
        dpre,
        moved(wide, spread, bins).astype(jnp.bfloat16),
    )
    dact = jnp.zeros(dy.shape, jnp.float32)
    for tap in range(3):
        dact = dact + jnp.dot(
            spans[tap], weight_ref[0, tap], preferred_element_type=jnp.float32
        )
    return (dy.astype(jnp.float32) + dact * x_slope).astype(jnp.bfloat16)


def of_seq(ref, seq, bins):
    if ref.shape[0] == bins:
        return ref[...]
    return ref[seq * bins : (seq + 1) * bins, :]


def split_kernel(last, payload_ref, *out_refs):
    count = len(out_refs)
    seq_count, bins, chans = payload_ref.shape
    part = bins // count
    section = lax.axis_index("pipe")
    place = lax.axis_index("ctx")

    @pl.when((section == 0) | (section == last))
    def send():
        source = payload_ref[...].reshape(seq_count * bins, chans)
        row = lax.broadcasted_iota(jnp.int32, (part, seq_count * bins), 0)
        col = lax.broadcasted_iota(jnp.int32, (part, seq_count * bins), 1)
        for hop in range(count):
            residue = lax.rem(place + hop, count)
            rows = [
                (col == seq * bins + count * row + residue).astype(jnp.float32)
                for seq in range(seq_count)
            ]
            pick = jnp.concatenate(rows, axis=0).astype(jnp.bfloat16)
            out_refs[hop][...] = jnp.dot(
                pick, source, preferred_element_type=jnp.float32
            ).astype(jnp.bfloat16)


def hold_kernel(weight_ref, point_ref, weight_out, point_out, sems):
    loads = [
        pltpu.make_async_copy(weight_ref, weight_out, sems.at[0]),
        pltpu.make_async_copy(point_ref, point_out, sems.at[1]),
    ]
    for load in loads:
        load.start()
    for load in loads:
        load.wait()


def first_kernel(last, bins, steps, *refs):
    parts, (weight_ref, point_ref, whole_ref, out_ref, pre_ref) = refs[:-5], refs[-5:]
    count = len(parts)
    section = lax.axis_index("pipe")
    place = lax.axis_index("ctx")
    part = bins // count
    seq_count = whole_ref.shape[0] // bins

    @pl.when((section == 0) | (section == last))
    def gather():
        for step, part_ref in zip(steps, parts):
            source = lax.rem(place + count - step, count)
            for seq in range(seq_count):
                at = pl.multiple_of(seq * bins + source * part, part)
                whole_ref[pl.ds(at, part), :] = part_ref[seq * part : (seq + 1) * part, :]

    @pl.when(section == 0)
    def layer():
        x = whole_ref[:bins, :]
        finish(x, fore(x, weight_ref, 1, bins), point_ref, out_ref, pre_ref)


def finish(x, pre, point_ref, out_ref, pre_ref):
    pre_ref[...] = pre
    branch = jnp.dot(
        gelu(pre).astype(jnp.bfloat16), point_ref[0], preferred_element_type=jnp.float32
    )
    out_ref[...] = (x.astype(jnp.float32) + branch).astype(jnp.bfloat16)


def fore_kernel(level, seq, bins, x_ref, weight_ref, point_ref, out_ref, pre_ref):
    @pl.when(lax.axis_index("pipe") == level)
    def layer():
        x = of_seq(x_ref, seq, bins)
        finish(x, fore(x, weight_ref, 2**level, bins), point_ref, out_ref, pre_ref)


def transpose_kernel(weight_ref, point_ref, weight_out, point_out):
    for tap in range(weight_ref.shape[1]):
        weight_out[0, tap] = weight_ref[0, tap].T
    point_out[0] = point_ref[0].T


def turn_kernel(level, seq, bins, scale, x_ref, cot_ref, weight_ref, weight_t_ref, point_t_ref, dy_ref, dpre_ref):
    @pl.when(lax.axis_index("pipe") == level)
    def layer():
        x = of_seq(x_ref, seq, bins)
        pre = fore(x, weight_ref, 2**level, bins)
        cot = of_seq(cot_ref, seq, bins)
        dy = (cot.astype(jnp.float32) * scale).astype(jnp.bfloat16)
        dpre = back_pre(dy, gelu_slope(pre), point_t_ref)
        dpre_ref[...] = dpre
        x_slope = gelu_slope(x.astype(jnp.float32))
        dy_ref[...] = back_trunk(dy, dpre, x_slope, weight_t_ref, 2**level, bins)


def slope_kernel(levels, seq_count, bins, *refs):
    xs, pres = refs[: levels * seq_count], refs[levels * seq_count : 2 * levels * seq_count]
    outs = refs[2 * levels * seq_count :]
    for level in range(levels):

        @pl.when(lax.axis_index("pipe") == level)
        def layer(level=level):
            for seq in range(seq_count):
                x = of_seq(xs[level * seq_count + seq], seq, bins)
                outs[2 * seq][...] = gelu_slope(x.astype(jnp.float32))
                outs[2 * seq + 1][...] = gelu_slope(pres[level * seq_count + seq][...])


def back_kernel(level, bins, dy_in_ref, x_slope_ref, pre_slope_ref, weight_ref, point_ref, dy_ref, dpre_ref):
    @pl.when(lax.axis_index("pipe") == level)
    def layer():
        dy = dy_in_ref[...]
        dpre = back_pre(dy, pre_slope_ref[...], point_ref)
        dpre_ref[...] = dpre
        dy_ref[...] = back_trunk(dy, dpre, x_slope_ref[...], weight_ref, 2**level, bins)


def message_kernel(places, *refs):
    blocks, message_ref = refs[:-1], refs[-1]
    size = message_ref.shape[0] // len(places)
    for to, (ref, at) in enumerate(zip(blocks, places)):
        message_ref[to * size : (to + 1) * size, :] = ref[at * size : (at + 1) * size, :]


def head_kernel(sections, earlier, dy_in_ref, slope_ref, point_ref, *refs):
    others, before, out_ref = refs[: sections - 1], refs[sections - 1 : -1], refs[-1]
    section = lax.axis_index("pipe")
    bins = dy_in_ref.shape[0]
    for ref in before:
        out_ref[:earlier, :] = ref[...]

    @pl.when(section == 0)
    def layer():
        out_ref[earlier : earlier + bins, :] = back_pre(dy_in_ref[...], slope_ref[...], point_ref)

    for level in range(1, sections):

        @pl.when(section == level)
        def keep(level=level):
            out_ref[earlier : earlier + bins, :] = others[level - 1][...]


def columns_kernel(groups, runs, kept, *refs):
    refs, (sent_ref,) = refs[:-1], refs[-1:]
    kept_refs = refs[sum(runs) :]
    count = 2 * len(kept)
    section = lax.axis_index("pipe")
    core = lax.axis_index("dp")
    place = lax.axis_index("ctx")
    x, start = None, 0
    for level, run in enumerate(runs):
        pieces = [ref[...] for ref in refs[start : start + run]]
        start += run
        whole = jnp.concatenate(pieces, axis=0).astype(jnp.float32)
        x = whole if x is None else jnp.where(section == level, whole, x)
    act = gelu(x).astype(jnp.bfloat16)
    chans = act.shape[1]
    width = chans // (groups * count)
    row = lax.broadcasted_iota(jnp.int32, (width, chans), 0)
    col = lax.broadcasted_iota(jnp.int32, (width, chans), 1)

    def block(offset):
        owner = lax.bitwise_xor(place, offset)
        rows = []
        for step in range(groups):
            first = (lax.rem(core + step, groups) * count + owner) * width
            rows.append((col == first + row).astype(jnp.float32))
        pick = jnp.concatenate(rows, axis=0).astype(jnp.bfloat16)
        return lax.dot_general(
            pick, act, contract_last, preferred_element_type=jnp.float32
        ).astype(jnp.bfloat16)

    size = groups * width
    for at, offset in enumerate(kept):
        kept_refs[at][...] = block(offset)
        sent_ref[at * size : (at + 1) * size, :] = block(offset ^ 1)


def grad_kernel(sections, bins, places, *refs):
    columns, refs = refs[: len(places)], refs[len(places) :]
    grads, out_ref = refs[:-1], refs[-1]
    section = lax.axis_index("pipe")
    width = out_ref.shape[1]

    def taps(spread):
        act = jnp.concatenate(
            [ref[at : at + width, :] for ref, at in zip(columns, places)], axis=1
        )
        dpre = jnp.concatenate([ref[...] for ref in grads], axis=0)
        wide = dpre.astype(jnp.float32)
        spans = (
            moved(wide, -spread, bins).astype(jnp.bfloat16),
            dpre,
            moved(wide, spread, bins).astype(jnp.bfloat16),
        )
        for tap in range(3):
            out_ref[tap] = jnp.dot(
                act, spans[tap], preferred_element_type=jnp.float32
            ).astype(out_ref.dtype)

    for level in range(sections):

        @pl.when(section == level)
        def run(level=level):
            taps(2**level)


def kernel_call(body, outs, flops, name, waits=(), carries=(), in_spec=in_vmem, scratch=()):
    def call(*args):
        used, taken = len(args), len(args) + len(waits) + len(carries)

        def run(*refs):
            made = refs[taken : taken + len(outs)]
            body(*refs[:used], *made, *refs[taken + len(outs) + len(carries) :])

        moved_bytes = sum(math.prod(a.shape) * a.dtype.itemsize for a in (*args, *outs))
        return pl.pallas_call(
            run,
            out_shape=[*outs, *(jax.ShapeDtypeStruct(a.shape, a.dtype) for a in carries)],
            in_specs=[in_spec] * used + [anywhere] * (taken - used),
            out_specs=[in_vmem] * len(outs) + [anywhere] * len(carries),
            input_output_aliases={
                used + len(waits) + at: len(outs) + at for at in range(len(carries))
            },
            scratch_shapes=list(scratch),
            compiler_params=pltpu.CompilerParams(vmem_limit_bytes=24 * 2**20),
            cost_estimate=pl.CostEstimate(
                flops=flops, bytes_accessed=moved_bytes, transcendentals=0
            ),
            name=name,
        )(*args, *waits, *carries)

    return call


def residue_shards(inputs, cotangent, weight, point):
    sections = lax.axis_size("pipe")
    section = lax.axis_index("pipe")
    count = lax.axis_size("ctx")
    groups = lax.axis_size("dp")
    seq_count, bins, chans = inputs.shape
    inner = weight.shape[3]
    rows = seq_count * bins
    scale = 1.0 / math.sqrt(seq_count * groups * bins * count)
    last = sections - 1
    seqs = range(seq_count)
    layer_flops = 2 * bins * chans * inner * 4

    def shape(*dims, dtype=jnp.bfloat16):
        return jax.ShapeDtypeStruct(dims, dtype)

    def hop(value, source, target, third=None):
        sends = {source: target, target: source}
        if third is not None and third not in sends:
            sends.update({target: third, third: source})
        route = []
        for core in range(groups):
            for stage in range(sections):
                taker = core if stage in sends else (core + 1) % groups
                for i in range(count):
                    giver = (core * sections + stage) * count + i
                    route.append((giver, (taker * sections + sends.get(stage, stage)) * count + i))
        return lax.ppermute(value, ("dp", "pipe", "ctx"), route)

    def onward(value, step):
        return lax.ppermute(value, "ctx", [(i, (i + step) % count) for i in range(count)])

    def exchange(value, offset):
        return lax.ppermute(value, "ctx", [(i, i ^ offset) for i in range(count)])

    payload = jnp.where(section == last, cotangent, inputs)
    parts = kernel_call(
        functools.partial(split_kernel, last),
        [shape(rows // count, chans)] * count,
        10 * seq_count * layer_flops,
        "split",
    )(payload)
    weight, point = kernel_call(
        hold_kernel,
        [shape(*weight.shape), shape(*point.shape)],
        0,
        "hold",
        waits=[parts[0]],
        in_spec=anywhere,
        scratch=[pltpu.SemaphoreType.DMA((2,))],
    )(weight, point)
    steps = [1, *range(count - 1, 1, -1)]
    parts = [*(onward(parts[step], step) for step in steps), parts[0]]

    trunk, inside = shape(bins, chans), shape(bins, inner)
    inside_wide = shape(bins, inner, dtype=jnp.float32)
    whole, out, pre = kernel_call(
        functools.partial(first_kernel, last, bins, [*steps, 0]),
        [shape(rows, chans), trunk, inside_wide],
        layer_flops,
        "first",
    )(*parts, weight, point)
    outs, pres, xs, sent = [out], [[pre]], [[whole]], ()
    for level in range(last):
        if level > 0:
            third = last if level > 1 else None
            xs.append([hop(out, level - 1, level, third) for out in outs])
            outs = []
            pres.append([])
        for seq in range(len(outs), seq_count):
            out, pre = kernel_call(
                functools.partial(fore_kernel, level, seq, bins),
                [trunk, inside_wide],
                layer_flops,
                "fore",
                waits=outs[-1:] or sent,
            )(xs[level][seq if level else 0], weight, point)
            outs.append(out)
            pres[level].append(pre)
        sent = outs
        if level == 1:
            back_weights = kernel_call(
                transpose_kernel,
                [shape(1, weight.shape[1], inner, chans), shape(1, chans, inner)],
                0,
                "transpose",
                waits=outs,
            )(weight, point)
            sent = [*outs, *back_weights]
    slopes = kernel_call(
        functools.partial(slope_kernel, last, seq_count, bins),
        [shape(bins, chans, dtype=jnp.float32), inside_wide] * seq_count,
        0,
        "slopes",
        waits=outs,
    )(
        *[xs[level][seq if level else 0] for level in range(last) for seq in seqs],
        *[pre for some in pres for pre in some],
    )
    sent = [*sent, *slopes]
    xs.append([hop(out, last - 1, last, 0) for out in outs])

    dys, dpres = [], [[] for level in range(sections)]
    for seq in seqs:
        dy, dpre = kernel_call(
            functools.partial(turn_kernel, last, seq, bins, scale),
            [trunk, inside],
            2 * layer_flops,
            "turn",
            waits=dys[-1:] or sent,
        )(xs[last][seq], whole, weight, *back_weights)
        dys.append(dy)
        dpres[last].append(dpre)
    kept = list(range(0, count, 2))
    moving = [(offset, 0) for offset in range(1, count, 2)]
    size = chans // count
    *owned, message = kernel_call(
        functools.partial(columns_kernel, groups, [len(x) for x in xs], kept),
        [shape(size, rows)] * len(kept) + [shape(size * len(kept), rows)],
        2 * rows * chans * chans,
        "columns",
        waits=dys,
    )(*[x for some in xs for x in some])
    blocks = {(offset, 0): (array, 0) for offset, array in zip(kept, owned)}
    sent = [owned[0]]
    dys = [hop(dy, last, last - 1) for dy in dys]
    message, bit = exchange(message, 1), 1
    blocks.update({(to ^ 1, start ^ 1): (message, at) for at, (to, start) in enumerate(moving)})

    for level in range(last - 1, 0, -1):
        outs = []
        for seq in seqs:
            dy, dpre = kernel_call(
                functools.partial(back_kernel, level, bins),
                [trunk, inside],
                layer_flops,
                "back",
                waits=outs[-1:] or sent,
            )(dys[seq], *slopes[2 * seq : 2 * seq + 2], *back_weights)
            outs.append(dy)
            dpres[level].append(dpre)
        sent = outs
        dys = [hop(dy, level, level - 1, None if level > 1 else last) for dy in outs]
        bit *= 2
        moving = sorted(key for key in blocks if key[0] & bit)
        if moving:
            (message,) = kernel_call(
                functools.partial(message_kernel, [blocks[key][1] for key in moving]),
                [shape(size * len(moving), rows)],
                0,
                "message",
                waits=outs,
            )(*[blocks[key][0] for key in moving])
            sent = [*outs, message]
            message = exchange(message, bit)
            for at, (to, start) in enumerate(moving):
                blocks[to ^ bit, start ^ bit] = (message, at)

    sent = [*sent, message]
    dpre = []
    for seq in seqs:
        dpre = kernel_call(
            functools.partial(head_kernel, sections, seq * bins),
            [shape((seq + 1) * bins, inner)],
            layer_flops // 4,
            "head",
            waits=dpre or sent,
        )(dys[seq], slopes[2 * seq + 1], back_weights[1], *[dpres[level][seq] for level in range(1, sections)], *dpre)
    (dpre,) = dpre
    received, bit = {0: dpre}, count // 2
    while bit:
        received.update({offset ^ bit: exchange(block, bit) for offset, block in received.items()})
        bit //= 2
    offsets = [*received]
    gathered = [received[offset] for offset in offsets]
    columns = [blocks[0, offset] for offset in offsets]
    width = size // groups

    def gradient(step, dtype, waits=()):
        places = [at * size + step * width for array, at in columns]
        (part,) = kernel_call(
            functools.partial(grad_kernel, sections, bins, places),
            [shape(3, width, inner, dtype=dtype)],
            2 * 3 * rows * count * width * inner,
            "grad",
            waits=waits,
        )(*[array for array, at in columns], *gathered)
        return part

    others = [gradient(step, jnp.bfloat16) for step in range(1, groups)]
    mine = gradient(0, jnp.float32, waits=others)
    for step, other in enumerate(others, 1):
        route = [(i, (i + step) % groups) for i in range(groups)]
        mine = mine + lax.ppermute(other, "dp", route).astype(jnp.float32)
    return mine[None]


def solution(mesh):
    def shards(inputs, cotangent, dilated_kernel_weight, point_weight):
        bins = inputs.shape[1]
        first_spread = bins // 2 // 2 ** (mesh.shape["pipe"] - 1)
        count = mesh.shape["ctx"]
        residues = (
            first_spread == count
            and mesh.shape["pipe"] > 2
            and bins % (16 * count) == 0
            and 1 < count == 1 << (count.bit_length() - 1) <= 1 << (mesh.shape["pipe"] - 2)
            and inputs.shape[2] % (count * mesh.shape["dp"]) == 0
        )
        plan = residue_shards if residues else edge_shards
        return plan(inputs, cotangent, dilated_kernel_weight, point_weight)

    return jax.shard_map(
        shards,
        mesh=mesh,
        in_specs=(
            P("dp", "ctx", None),
            P("dp", "ctx", None),
            P("pipe", None, None, None),
            P("pipe", None, None),
        ),
        out_specs=P("pipe", None, ("dp", "ctx"), None),
        check_vma=False,
    )
```

profile of v0, /device:TPU:0, one launch (start us, length us, event | category | flops | bytes accessed | tf_op | source)
XLA Modules:
  0.0 58.0 jit_solution(11546681884130953522)
XLA Ops:
  0.0 1.0 %broadcast_select_fusion.refs_0_ = bf16[2,64,768]{2,1,0:T(8,128)(2,1)S(1)} fusion(bf16[2,64,768]{2,1,0:T(8,128)(2,1)} %param.5, bf16[2,64,768]{2,1,0:T(8,128)(2,1)} %param.4, pred[]{:T(512)S(6)} %eq.3), kind=kLoop, calls=%fused_computation.1 | loop fusion | flops 98304 | bytes 589825 | tf_op jit(solution)/shard_map/jit(_where)/select_n | solution.py:475
  1.2 3.1 %collective-permute-start = (bf16[32,768]{1,0:T(8,128)(2,1)S(1)}, bf16[32,768]{1,0:T(8,128)(2,1)S(1)}, u32[]{:S(2)}, u32[]{:S(2)}) collective-permute-start(bf16[32,768]{1,0:T(8,128)(2,1)S(1)} %get-tuple-element.45), channel_id=1, source_target_pairs={{0,1},{1,2},{2,3},{3,0},{4,5},{5,6},{6,7},{7,4},{8,9},{9,10},{10,1... | collective-permute-start | bytes 147464 | tf_op jit(solution)/shard_map/ppermute | solution.py:470
  4.3 2.1 %collective-permute-start.1 = (bf16[32,768]{1,0:T(8,128)(2,1)S(1)}, bf16[32,768]{1,0:T(8,128)(2,1)S(1)}, u32[]{:S(2)}, u32[]{:S(2)}) collective-permute-start(bf16[32,768]{1,0:T(8,128)(2,1)S(1)} %get-tuple-element.46), channel_id=1, source_target_pairs={{0,3},{1,0},{2,1},{3,2},{4,7},{5,4},{6,5},{7,6},{8,11},{9,8},{10,9... | collective-permute-start | bytes 147464 | tf_op jit(solution)/shard_map/ppermute | solution.py:470
  6.4 0.9 %collective-permute-start.2 = (bf16[32,768]{1,0:T(8,128)(2,1)S(1)}, bf16[32,768]{1,0:T(8,128)(2,1)S(1)}, u32[]{:S(2)}, u32[]{:S(2)}) collective-permute-start(bf16[32,768]{1,0:T(8,128)(2,1)S(1)} %get-tuple-element.47), channel_id=1, source_target_pairs={{0,2},{1,3},{2,0},{3,1},{4,6},{5,7},{6,4},{7,5},{8,10},{9,11},{10,... | collective-permute-start | bytes 147464 | tf_op jit(solution)/shard_map/ppermute | solution.py:470
  7.3 0.5 hold.1
  7.8 0.7 %collective-permute-done.refs_0_ = bf16[32,768]{1,0:T(8,128)(2,1)S(1)} collective-permute-done((bf16[32,768]{1,0:T(8,128)(2,1)S(1)}, bf16[32,768]{1,0:T(8,128)(2,1)S(1)}, u32[]{:S(2)}, u32[]{:S(2)}) %collective-permute-start) | collective-permute-done | bytes 49184 | tf_op jit(solution)/shard_map/ppermute | solution.py:470
  8.9 2.6 %collective-permute-done.2.refs_2_ = bf16[32,768]{1,0:T(8,128)(2,1)S(1)} collective-permute-done((bf16[32,768]{1,0:T(8,128)(2,1)S(1)}, bf16[32,768]{1,0:T(8,128)(2,1)S(1)}, u32[]{:S(2)}, u32[]{:S(2)}) %collective-permute-start.2) | collective-permute-done | bytes 49184 | tf_op jit(solution)/shard_map/ppermute | solution.py:470
  11.5 0.6 %first.1 = (bf16[128,768]{1,0:T(8,128)(2,1)S(1)}, bf16[64,768]{1,0:T(8,128)(2,1)S(1)}, f32[64,384]{1,0:T(8,128)S(1)}) custom-call(bf16[32,768]{1,0:T(8,128)(2,1)S(1)} %collective-permute-done.refs_0_, bf16[32,768]{1,0:T(8,128)(2,1)S(1)} %collective-permute-done.1.refs_1_, bf16[32,768]{1,0:T(8,128)(2,1)S(1)} %collective-permute-done.2.refs_2_, ...), custom_call_target="tpu_custom_call" | custom-call | flops 150994944 | bytes 2949120 | tf_op jit(solution)/shard_map/first/pallas_call | solution.py:421
  12.2 0.7 %collective-permute-start.3 = (bf16[64,768]{1,0:T(8,128)(2,1)S(1)}, bf16[64,768]{1,0:T(8,128)(2,1)S(1)}, u32[]{:S(2)}, u32[]{:S(2)}) collective-permute-start(bf16[64,768]{1,0:T(8,128)(2,1)S(1)} %get-tuple-element.52.refs_3_), channel_id=1, source_target_pairs={{0,4},{1,5},{2,6},{3,7},{4,0},{5,1},{6,2},{7,3},{8,24},{9,25},{10,... | collective-permute-start | bytes 294920 | tf_op jit(solution)/shard_map/ppermute | solution.py:467
  12.8 0.6 %fore.5 = (bf16[64,768]{1,0:T(8,128)(2,1)S(1)}, f32[64,384]{1,0:T(8,128)S(1)}) custom-call(bf16[128,768]{1,0:T(8,128)(2,1)S(1)} %get-tuple-element.51.refs_0_.refs_1_, bf16[1,3,768,384]{3,2,1,0:T(8,128)(2,1)S(1)} %get-tuple-element.49.refs_4_.refs_1_.refs_0_.refs_2_, bf16[1,384,768]{2,1,0:T(8,128)(2,1)S(1)} %get-tuple-element.50.refs_5_.refs_2_.refs_1_, ...), custom_call_target="tpu_custom_call" | custom-call | flops 150994944 | bytes 2752512 | tf_op jit(solution)/shard_map/fore/pallas_call | solution.py:421
  13.4 0.8 %collective-permute-start.4 = (bf16[64,768]{1,0:T(8,128)(2,1)S(1)}, bf16[64,768]{1,0:T(8,128)(2,1)S(1)}, u32[]{:S(2)}, u32[]{:S(2)}) collective-permute-start(bf16[64,768]{1,0:T(8,128)(2,1)S(1)} %get-tuple-element.53.refs_4_), channel_id=1, source_target_pairs={{0,4},{1,5},{2,6},{3,7},{4,0},{5,1},{6,2},{7,3},{8,24},{9,25},{10,... | collective-permute-start | bytes 294920 | tf_op jit(solution)/shard_map/ppermute | solution.py:467
  14.3 2.9 %collective-permute-done.3.refs_0_.refs_2_.refs_1_ = bf16[64,768]{1,0:T(8,128)(2,1)S(1)} collective-permute-done((bf16[64,768]{1,0:T(8,128)(2,1)S(1)}, bf16[64,768]{1,0:T(8,128)(2,1)S(1)}, u32[]{:S(2)}, u32[]{:S(2)}) %collective-permute-start.3) | collective-permute-done | bytes 98336 | tf_op jit(solution)/shard_map/ppermute | solution.py:467
  17.2 2.1 %collective-permute-done.4.refs_0_.refs_3_.refs_2_ = bf16[64,768]{1,0:T(8,128)(2,1)S(1)} collective-permute-done((bf16[64,768]{1,0:T(8,128)(2,1)S(1)}, bf16[64,768]{1,0:T(8,128)(2,1)S(1)}, u32[]{:S(2)}, u32[]{:S(2)}) %collective-permute-start.4) | collective-permute-done | bytes 98336 | tf_op jit(solution)/shard_map/ppermute | solution.py:467
  19.3 0.7 %transpose.1 = (bf16[1,3,384,768]{3,2,1,0:T(8,128)(2,1)S(1)}, bf16[1,768,384]{2,1,0:T(8,128)(2,1)S(1)}) custom-call(bf16[1,3,768,384]{3,2,1,0:T(8,128)(2,1)S(1)} %get-tuple-element.49.refs_4_.refs_1_.refs_0_.refs_2_, bf16[1,384,768]{2,1,0:T(8,128)(2,1)S(1)} %get-tuple-element.50.refs_5_.refs_2_.refs_1_, ...), custom_call_target="tpu_custom_call" | custom-call | bytes 4718592 | tf_op jit(solution)/shard_map/transpose/pallas_call | solution.py:421
  20.0 3.2 %collective-permute-start.7 = (bf16[64,768]{1,0:T(8,128)(2,1)S(1)}, bf16[64,768]{1,0:T(8,128)(2,1)S(1)}, u32[]{:S(2)}, u32[]{:S(2)}) collective-permute-start(bf16[64,768]{1,0:T(8,128)(2,1)S(1)} %get-tuple-element.58.refs_3_.refs_12_.refs_5_), channel_id=1, source_target_pairs={{0,8},{1,9},{2,10},{3,11},{4,20},{5,21},{6,22},{7,23},{8,12},{9,13... | collective-permute-start | bytes 294920 | tf_op jit(solution)/shard_map/ppermute | solution.py:467
  23.2 1.1 %collective-permute-start.8 = (bf16[64,768]{1,0:T(8,128)(2,1)S(1)}, bf16[64,768]{1,0:T(8,128)(2,1)S(1)}, u32[]{:S(2)}, u32[]{:S(2)}) collective-permute-start(bf16[64,768]{1,0:T(8,128)(2,1)S(1)} %get-tuple-element.59.refs_13_.refs_6_), channel_id=1, source_target_pairs={{0,8},{1,9},{2,10},{3,11},{4,20},{5,21},{6,22},{7,23},{8,12},{9,13... | collective-permute-start | bytes 294920 | tf_op jit(solution)/shard_map/ppermute | solution.py:467
  24.6 1.9 %collective-permute-done.7.refs_0_.refs_5_ = bf16[64,768]{1,0:T(8,128)(2,1)S(1)} collective-permute-done((bf16[64,768]{1,0:T(8,128)(2,1)S(1)}, bf16[64,768]{1,0:T(8,128)(2,1)S(1)}, u32[]{:S(2)}, u32[]{:S(2)}) %collective-permute-start.7) | collective-permute-done | bytes 98336 | tf_op jit(solution)/shard_map/ppermute | solution.py:467
  26.5 2.9 %collective-permute-done.8.refs_0_.refs_6_ = bf16[64,768]{1,0:T(8,128)(2,1)S(1)} collective-permute-done((bf16[64,768]{1,0:T(8,128)(2,1)S(1)}, bf16[64,768]{1,0:T(8,128)(2,1)S(1)}, u32[]{:S(2)}, u32[]{:S(2)}) %collective-permute-start.8) | collective-permute-done | bytes 98336 | tf_op jit(solution)/shard_map/ppermute | solution.py:467
  29.5 0.6 columns.1
  30.9 4.4 %collective-permute-done.9.refs_1_.refs_2_ = bf16[384,128]{1,0:T(8,128)(2,1)S(1)} collective-permute-done((bf16[384,128]{1,0:T(8,128)(2,1)S(1)}, bf16[384,128]{1,0:T(8,128)(2,1)S(1)}, u32[]{:S(2)}, u32[]{:S(2)}) %collective-permute-start.9) | collective-permute-done | bytes 98336 | tf_op jit(solution)/shard_map/ppermute | solution.py:473
  35.3 1.4 %collective-permute-start.12 = (bf16[384,128]{1,0:T(8,128)(2,1)S(1)}, bf16[384,128]{1,0:T(8,128)(2,1)S(1)}, u32[]{:S(2)}, u32[]{:S(2)}) collective-permute-start(bf16[384,128]{1,0:T(8,128)(2,1)S(1)} %message.1.refs_7_), channel_id=1, source_target_pairs={{0,2},{1,3},{2,0},{3,1},{4,6},{5,7},{6,4},{7,5},{8,10},{9,11},{10,... | collective-permute-start | bytes 294920 | tf_op jit(solution)/shard_map/ppermute | solution.py:473
  36.8 1.6 %collective-permute-start.16 = (bf16[64,768]{1,0:T(8,128)(2,1)S(1)}, bf16[64,768]{1,0:T(8,128)(2,1)S(1)}, u32[]{:S(2)}, u32[]{:S(2)}) collective-permute-start(bf16[64,768]{1,0:T(8,128)(2,1)S(1)} %get-tuple-element.77.refs_5_.refs_6_), channel_id=1, source_target_pairs={{0,12},{1,13},{2,14},{3,15},{4,0},{5,1},{6,2},{7,3},{8,24},{9,25},... | collective-permute-start | bytes 294920 | tf_op jit(solution)/shard_map/ppermute | solution.py:467
  38.4 3.1 %collective-permute-start.15 = (bf16[64,768]{1,0:T(8,128)(2,1)S(1)}, bf16[64,768]{1,0:T(8,128)(2,1)S(1)}, u32[]{:S(2)}, u32[]{:S(2)}) collective-permute-start(bf16[64,768]{1,0:T(8,128)(2,1)S(1)} %get-tuple-element.78.refs_7_), channel_id=1, source_target_pairs={{0,12},{1,13},{2,14},{3,15},{4,0},{5,1},{6,2},{7,3},{8,24},{9,25},... | collective-permute-start | bytes 294920 | tf_op jit(solution)/shard_map/ppermute | solution.py:467
  41.4 1.3 %collective-permute-done.12.refs_8_.refs_1_.refs_3_ = bf16[384,128]{1,0:T(8,128)(2,1)S(1)} collective-permute-done((bf16[384,128]{1,0:T(8,128)(2,1)S(1)}, bf16[384,128]{1,0:T(8,128)(2,1)S(1)}, u32[]{:S(2)}, u32[]{:S(2)}) %collective-permute-start.12) | collective-permute-done | bytes 98336 | tf_op jit(solution)/shard_map/ppermute | solution.py:473
  43.1 0.8 %collective-permute-done.15.refs_0_ = bf16[64,768]{1,0:T(8,128)(2,1)S(1)} collective-permute-done((bf16[64,768]{1,0:T(8,128)(2,1)S(1)}, bf16[64,768]{1,0:T(8,128)(2,1)S(1)}, u32[]{:S(2)}, u32[]{:S(2)}) %collective-permute-start.15) | collective-permute-done | bytes 98336 | tf_op jit(solution)/shard_map/ppermute | solution.py:467
  44.1 3.5 %collective-permute-start.17 = (bf16[128,384]{1,0:T(8,128)(2,1)S(1)}, bf16[128,384]{1,0:T(8,128)(2,1)S(1)}, u32[]{:S(2)}, u32[]{:S(2)}) collective-permute-start(bf16[128,384]{1,0:T(8,128)(2,1)S(1)} %head.3.refs_4_), channel_id=1, source_target_pairs={{0,2},{1,3},{2,0},{3,1},{4,6},{5,7},{6,4},{7,5},{8,10},{9,11},{10,... | collective-permute-start | bytes 294920 | tf_op jit(solution)/shard_map/ppermute | solution.py:473
  47.7 3.0 %collective-permute-done.17.refs_5_ = bf16[128,384]{1,0:T(8,128)(2,1)S(1)} collective-permute-done((bf16[128,384]{1,0:T(8,128)(2,1)S(1)}, bf16[128,384]{1,0:T(8,128)(2,1)S(1)}, u32[]{:S(2)}, u32[]{:S(2)}) %collective-permute-start.17) | collective-permute-done | bytes 98336 | tf_op jit(solution)/shard_map/ppermute | solution.py:473
  50.6 1.4 %collective-permute-start.19 = (bf16[128,384]{1,0:T(8,128)(2,1)S(1)}, bf16[128,384]{1,0:T(8,128)(2,1)S(1)}, u32[]{:S(2)}, u32[]{:S(2)}) collective-permute-start(bf16[128,384]{1,0:T(8,128)(2,1)S(1)} %collective-permute-done.17.refs_5_), channel_id=1, source_target_pairs={{0,1},{1,0},{2,3},{3,2},{4,5},{5,4},{6,7},{7,6},{8,9},{9,8},{10,11... | collective-permute-start | bytes 294920 | tf_op jit(solution)/shard_map/ppermute | solution.py:473
  52.1 0.7 %collective-permute-done.18.refs_6_ = bf16[128,384]{1,0:T(8,128)(2,1)S(1)} collective-permute-done((bf16[128,384]{1,0:T(8,128)(2,1)S(1)}, bf16[128,384]{1,0:T(8,128)(2,1)S(1)}, u32[]{:S(2)}, u32[]{:S(2)}) %collective-permute-start.18) | collective-permute-done | bytes 98336 | tf_op jit(solution)/shard_map/ppermute | solution.py:473
  52.8 2.5 %collective-permute-done.19.refs_7_ = bf16[128,384]{1,0:T(8,128)(2,1)S(1)} collective-permute-done((bf16[128,384]{1,0:T(8,128)(2,1)S(1)}, bf16[128,384]{1,0:T(8,128)(2,1)S(1)}, u32[]{:S(2)}, u32[]{:S(2)}) %collective-permute-start.19) | collective-permute-done | bytes 98336 | tf_op jit(solution)/shard_map/ppermute | solution.py:473
  56.1 1.1 %collective-permute-done.20 = bf16[3,96,384]{2,1,0:T(8,128)(2,1)S(1)} collective-permute-done((bf16[3,96,384]{2,1,0:T(8,128)(2,1)S(1)}, bf16[3,96,384]{2,1,0:T(8,128)(2,1)S(1)}, u32[]{:S(2)}, u32[]{:S(2)}) %collective-permute-start.20) | collective-permute-done | bytes 221216 | tf_op jit(solution)/shard_map/ppermute | solution.py:633
  57.2 0.8 %add_bitcast_fusion = f32[1,3,96,384]{3,2,1,0:T(8,128)} fusion(f32[3,96,384]{2,1,0:T(8,128)S(1)} %grad.3, bf16[3,96,384]{2,1,0:T(8,128)(2,1)S(1)} %collective-permute-done.20), kind=kLoop, calls=%fused_computation | loop fusion | flops 221184 | bytes 1105920 | tf_op jit(solution)/shard_map/broadcast_in_dim | solution.py:634
  (38 shorter events, 3.3 us)
Async XLA Ops:
  1.0 6.4 %copy-start = (bf16[1,3,768,384]{3,2,1,0:T(8,128)(2,1)S(1)}, bf16[1,3,768,384]{3,2,1,0:T(8,128)(2,1)}, u32[]{:S(2)}) copy-start(bf16[1,3,768,384]{3,2,1,0:T(8,128)(2,1)} %refs_0_.1) | copy-start | bytes 5308420
  1.0 6.4 %copy-start.1 = (bf16[1,384,768]{2,1,0:T(8,128)(2,1)S(1)}, bf16[1,384,768]{2,1,0:T(8,128)(2,1)}, u32[]{:S(2)}) copy-start(bf16[1,384,768]{2,1,0:T(8,128)(2,1)} %refs_1_.1) | copy-start | bytes 1769476
  1.2 7.3 %collective-permute-start = (bf16[32,768]{1,0:T(8,128)(2,1)S(1)}, bf16[32,768]{1,0:T(8,128)(2,1)S(1)}, u32[]{:S(2)}, u32[]{:S(2)}) collective-permute-start(bf16[32,768]{1,0:T(8,128)(2,1)S(1)} %get-tuple-element.45), channel_id=1, source_target_pairs={{0,1},{1,2},{2,3},{3,0},{4,5},{5,6},{6,7},{7,4},{8,9},{9,10},{10,1... | collective-permute-start | bytes 147464 | tf_op jit(solution)/shard_map/ppermute | solution.py:470
  4.3 4.6 %collective-permute-start.1 = (bf16[32,768]{1,0:T(8,128)(2,1)S(1)}, bf16[32,768]{1,0:T(8,128)(2,1)S(1)}, u32[]{:S(2)}, u32[]{:S(2)}) collective-permute-start(bf16[32,768]{1,0:T(8,128)(2,1)S(1)} %get-tuple-element.46), channel_id=1, source_target_pairs={{0,3},{1,0},{2,1},{3,2},{4,7},{5,4},{6,5},{7,6},{8,11},{9,8},{10,9... | collective-permute-start | bytes 147464 | tf_op jit(solution)/shard_map/ppermute | solution.py:470
  6.4 5.1 %collective-permute-start.2 = (bf16[32,768]{1,0:T(8,128)(2,1)S(1)}, bf16[32,768]{1,0:T(8,128)(2,1)S(1)}, u32[]{:S(2)}, u32[]{:S(2)}) collective-permute-start(bf16[32,768]{1,0:T(8,128)(2,1)S(1)} %get-tuple-element.47), channel_id=1, source_target_pairs={{0,2},{1,3},{2,0},{3,1},{4,6},{5,7},{6,4},{7,5},{8,10},{9,11},{10,... | collective-permute-start | bytes 147464 | tf_op jit(solution)/shard_map/ppermute | solution.py:470
  12.2 5.0 %collective-permute-start.3 = (bf16[64,768]{1,0:T(8,128)(2,1)S(1)}, bf16[64,768]{1,0:T(8,128)(2,1)S(1)}, u32[]{:S(2)}, u32[]{:S(2)}) collective-permute-start(bf16[64,768]{1,0:T(8,128)(2,1)S(1)} %get-tuple-element.52.refs_3_), channel_id=1, source_target_pairs={{0,4},{1,5},{2,6},{3,7},{4,0},{5,1},{6,2},{7,3},{8,24},{9,25},{10,... | collective-permute-start | bytes 294920 | tf_op jit(solution)/shard_map/ppermute | solution.py:467
  13.4 5.8 %collective-permute-start.4 = (bf16[64,768]{1,0:T(8,128)(2,1)S(1)}, bf16[64,768]{1,0:T(8,128)(2,1)S(1)}, u32[]{:S(2)}, u32[]{:S(2)}) collective-permute-start(bf16[64,768]{1,0:T(8,128)(2,1)S(1)} %get-tuple-element.53.refs_4_), channel_id=1, source_target_pairs={{0,4},{1,5},{2,6},{3,7},{4,0},{5,1},{6,2},{7,3},{8,24},{9,25},{10,... | collective-permute-start | bytes 294920 | tf_op jit(solution)/shard_map/ppermute | solution.py:467
  17.1 2.8 %collective-permute-start.5 = (bf16[64,768]{1,0:T(8,128)(2,1)S(1)}, bf16[64,768]{1,0:T(8,128)(2,1)S(1)}, u32[]{:S(2)}, u32[]{:S(2)}) collective-permute-start(bf16[64,768]{1,0:T(8,128)(2,1)S(1)} %get-tuple-element.54.refs_3_.refs_2_), channel_id=1, source_target_pairs={{0,16},{1,17},{2,18},{3,19},{4,8},{5,9},{6,10},{7,11},{8,12},{9,13... | collective-permute-start | bytes 294920 | tf_op jit(solution)/shard_map/ppermute | solution.py:467
  19.3 3.9 %collective-permute-start.6 = (bf16[64,768]{1,0:T(8,128)(2,1)S(1)}, bf16[64,768]{1,0:T(8,128)(2,1)S(1)}, u32[]{:S(2)}, u32[]{:S(2)}) collective-permute-start(bf16[64,768]{1,0:T(8,128)(2,1)S(1)} %get-tuple-element.55.refs_3_.refs_4_), channel_id=1, source_target_pairs={{0,16},{1,17},{2,18},{3,19},{4,8},{5,9},{6,10},{7,11},{8,12},{9,13... | collective-permute-start | bytes 294920 | tf_op jit(solution)/shard_map/ppermute | solution.py:467
  20.0 6.5 %collective-permute-start.7 = (bf16[64,768]{1,0:T(8,128)(2,1)S(1)}, bf16[64,768]{1,0:T(8,128)(2,1)S(1)}, u32[]{:S(2)}, u32[]{:S(2)}) collective-permute-start(bf16[64,768]{1,0:T(8,128)(2,1)S(1)} %get-tuple-element.58.refs_3_.refs_12_.refs_5_), channel_id=1, source_target_pairs={{0,8},{1,9},{2,10},{3,11},{4,20},{5,21},{6,22},{7,23},{8,12},{9,13... | collective-permute-start | bytes 294920 | tf_op jit(solution)/shard_map/ppermute | solution.py:467
  23.2 6.3 %collective-permute-start.8 = (bf16[64,768]{1,0:T(8,128)(2,1)S(1)}, bf16[64,768]{1,0:T(8,128)(2,1)S(1)}, u32[]{:S(2)}, u32[]{:S(2)}) collective-permute-start(bf16[64,768]{1,0:T(8,128)(2,1)S(1)} %get-tuple-element.59.refs_13_.refs_6_), channel_id=1, source_target_pairs={{0,8},{1,9},{2,10},{3,11},{4,20},{5,21},{6,22},{7,23},{8,12},{9,13... | collective-permute-start | bytes 294920 | tf_op jit(solution)/shard_map/ppermute | solution.py:467
  26.5 3.9 %collective-permute-start.10 = (bf16[64,768]{1,0:T(8,128)(2,1)S(1)}, bf16[64,768]{1,0:T(8,128)(2,1)S(1)}, u32[]{:S(2)}, u32[]{:S(2)}) collective-permute-start(bf16[64,768]{1,0:T(8,128)(2,1)S(1)} %get-tuple-element.70.refs_5_.refs_7_), channel_id=1, source_target_pairs={{0,16},{1,17},{2,18},{3,19},{4,20},{5,21},{6,22},{7,23},{8,12},{9,... | collective-permute-start | bytes 294920 | tf_op jit(solution)/shard_map/ppermute | solution.py:467
  29.5 1.3 %collective-permute-start.11 = (bf16[64,768]{1,0:T(8,128)(2,1)S(1)}, bf16[64,768]{1,0:T(8,128)(2,1)S(1)}, u32[]{:S(2)}, u32[]{:S(2)}) collective-permute-start(bf16[64,768]{1,0:T(8,128)(2,1)S(1)} %get-tuple-element.71.refs_8_), channel_id=1, source_target_pairs={{0,16},{1,17},{2,18},{3,19},{4,20},{5,21},{6,22},{7,23},{8,12},{9,... | collective-permute-start | bytes 294920 | tf_op jit(solution)/shard_map/ppermute | solution.py:467
  30.0 5.3 %collective-permute-start.9 = (bf16[384,128]{1,0:T(8,128)(2,1)S(1)}, bf16[384,128]{1,0:T(8,128)(2,1)S(1)}, u32[]{:S(2)}, u32[]{:S(2)}) collective-permute-start(bf16[384,128]{1,0:T(8,128)(2,1)S(1)} %get-tuple-element.74), channel_id=1, source_target_pairs={{0,1},{1,0},{2,3},{3,2},{4,5},{5,4},{6,7},{7,6},{8,9},{9,8},{10,11... | collective-permute-start | bytes 294920 | tf_op jit(solution)/shard_map/ppermute | solution.py:473
  30.4 6.4 %collective-permute-start.14 = (bf16[64,768]{1,0:T(8,128)(2,1)S(1)}, bf16[64,768]{1,0:T(8,128)(2,1)S(1)}, u32[]{:S(2)}, u32[]{:S(2)}) collective-permute-start(bf16[64,768]{1,0:T(8,128)(2,1)S(1)} %get-tuple-element.75.refs_5_.refs_2_), channel_id=1, source_target_pairs={{0,16},{1,17},{2,18},{3,19},{4,8},{5,9},{6,10},{7,11},{8,4},{9,5},... | collective-permute-start | bytes 294920 | tf_op jit(solution)/shard_map/ppermute | solution.py:467
  30.8 7.6 %collective-permute-start.13 = (bf16[64,768]{1,0:T(8,128)(2,1)S(1)}, bf16[64,768]{1,0:T(8,128)(2,1)S(1)}, u32[]{:S(2)}, u32[]{:S(2)}) collective-permute-start(bf16[64,768]{1,0:T(8,128)(2,1)S(1)} %get-tuple-element.76.refs_3_.refs_6_), channel_id=1, source_target_pairs={{0,16},{1,17},{2,18},{3,19},{4,8},{5,9},{6,10},{7,11},{8,4},{9,5},... | collective-permute-start | bytes 294920 | tf_op jit(solution)/shard_map/ppermute | solution.py:467
  35.3 7.4 %collective-permute-start.12 = (bf16[384,128]{1,0:T(8,128)(2,1)S(1)}, bf16[384,128]{1,0:T(8,128)(2,1)S(1)}, u32[]{:S(2)}, u32[]{:S(2)}) collective-permute-start(bf16[384,128]{1,0:T(8,128)(2,1)S(1)} %message.1.refs_7_), channel_id=1, source_target_pairs={{0,2},{1,3},{2,0},{3,1},{4,6},{5,7},{6,4},{7,5},{8,10},{9,11},{10,... | collective-permute-start | bytes 294920 | tf_op jit(solution)/shard_map/ppermute | solution.py:473
  36.8 6.1 %collective-permute-start.16 = (bf16[64,768]{1,0:T(8,128)(2,1)S(1)}, bf16[64,768]{1,0:T(8,128)(2,1)S(1)}, u32[]{:S(2)}, u32[]{:S(2)}) collective-permute-start(bf16[64,768]{1,0:T(8,128)(2,1)S(1)} %get-tuple-element.77.refs_5_.refs_6_), channel_id=1, source_target_pairs={{0,12},{1,13},{2,14},{3,15},{4,0},{5,1},{6,2},{7,3},{8,24},{9,25},... | collective-permute-start | bytes 294920 | tf_op jit(solution)/shard_map/ppermute | solution.py:467
  38.4 5.5 %collective-permute-start.15 = (bf16[64,768]{1,0:T(8,128)(2,1)S(1)}, bf16[64,768]{1,0:T(8,128)(2,1)S(1)}, u32[]{:S(2)}, u32[]{:S(2)}) collective-permute-start(bf16[64,768]{1,0:T(8,128)(2,1)S(1)} %get-tuple-element.78.refs_7_), channel_id=1, source_target_pairs={{0,12},{1,13},{2,14},{3,15},{4,0},{5,1},{6,2},{7,3},{8,24},{9,25},... | collective-permute-start | bytes 294920 | tf_op jit(solution)/shard_map/ppermute | solution.py:467
  44.1 6.5 %collective-permute-start.17 = (bf16[128,384]{1,0:T(8,128)(2,1)S(1)}, bf16[128,384]{1,0:T(8,128)(2,1)S(1)}, u32[]{:S(2)}, u32[]{:S(2)}) collective-permute-start(bf16[128,384]{1,0:T(8,128)(2,1)S(1)} %head.3.refs_4_), channel_id=1, source_target_pairs={{0,2},{1,3},{2,0},{3,1},{4,6},{5,7},{6,4},{7,5},{8,10},{9,11},{10,... | collective-permute-start | bytes 294920 | tf_op jit(solution)/shard_map/ppermute | solution.py:473
  47.6 5.1 %collective-permute-start.18 = (bf16[128,384]{1,0:T(8,128)(2,1)S(1)}, bf16[128,384]{1,0:T(8,128)(2,1)S(1)}, u32[]{:S(2)}, u32[]{:S(2)}) collective-permute-start(bf16[128,384]{1,0:T(8,128)(2,1)S(1)} %head.3.refs_4_), channel_id=1, source_target_pairs={{0,1},{1,0},{2,3},{3,2},{4,5},{5,4},{6,7},{7,6},{8,9},{9,8},{10,11... | collective-permute-start | bytes 294920 | tf_op jit(solution)/shard_map/ppermute | solution.py:473
  50.6 4.6 %collective-permute-start.19 = (bf16[128,384]{1,0:T(8,128)(2,1)S(1)}, bf16[128,384]{1,0:T(8,128)(2,1)S(1)}, u32[]{:S(2)}, u32[]{:S(2)}) collective-permute-start(bf16[128,384]{1,0:T(8,128)(2,1)S(1)} %collective-permute-done.17.refs_5_), channel_id=1, source_target_pairs={{0,1},{1,0},{2,3},{3,2},{4,5},{5,4},{6,7},{7,6},{8,9},{9,8},{10,11... | collective-permute-start | bytes 294920 | tf_op jit(solution)/shard_map/ppermute | solution.py:473
  55.6 1.5 %collective-permute-start.20 = (bf16[3,96,384]{2,1,0:T(8,128)(2,1)S(1)}, bf16[3,96,384]{2,1,0:T(8,128)(2,1)S(1)}, u32[]{:S(2)}, u32[]{:S(2)}) collective-permute-start(bf16[3,96,384]{2,1,0:T(8,128)(2,1)S(1)} %grad.2.refs_8_), channel_id=1, source_target_pairs={{0,16},{16,0},{1,17},{17,1},{2,18},{18,2},{3,19},{19,3},{4,20},{20... | collective-permute-start | bytes 663560 | tf_op jit(solution)/shard_map/ppermute | solution.py:633
where the time goes:
time: 58.1 us; the launch traced here: 58 us
  waiting for transfers between devices  27.4 us (47%)
  starting transfers between devices  23.9 us (41%)
  Pallas kernels  4.74 us (8%)
  other arithmetic  1.75 us (3%)
    ppermute x5, waiting for transfers between devices, exchange(): return lax.ppermute(value, 'ctx', [(i, i ^ offset) for i in range(count)])  11.8 us
    ppermute x12, starting transfers between devices, hop(): return lax.ppermute(value, ('dp', 'pipe', 'ctx'), route)  11 us
    ppermute x12, waiting for transfers between devices, hop(): return lax.ppermute(value, ('dp', 'pipe', 'ctx'), route)  10.9 us
    ppermute x5, starting transfers between devices, exchange(): return lax.ppermute(value, 'ctx', [(i, i ^ offset) for i in range(count)])  6.77 us
    ppermute x3, starting transfers between devices, onward(): lax.ppermute(value, 'ctx', [(i, (i + step) % count) for i in range(count)])  6.11 us
    pallas_call x22, Pallas kernels, call(): pl.pallas_call(run, out_shape=[*outs, *(jax.ShapeDtypeStruct(a.shape, a.d...  4.74 us
    ppermute x3, waiting for transfers between devices, onward(): lax.ppermute(value, 'ctx', [(i, (i + step) % count) for i in range(count)])  3.66 us
  transfers between devices with their start and end apart: 21, of which 15 were waited for; matrix products, arithmetic and copies ran while one was open for 0% of the time, Pallas kernels for 6%

commit v1 on v0

--- a/solution.py
+++ b/solution.py
@@ -579,7 +579,7 @@
             outs.append(dy)
             dpres[level].append(dpre)
         sent = outs
-        dys = [hop(dy, level, level - 1, None if level > 1 else last) for dy in outs]
+        dys = [hop(dy, level, level - 1, 0 if level > 1 else last) for dy in outs]
         bit *= 2
         moving = sorted(key for key in blocks if key[0] & bit)
         if moving:

time: 58.1 us -> 58.3 us (level)
  starting transfers between devices: 23.9 us -> 28.4 us
  waiting for transfers between devices: 27.4 us -> 23.1 us
    ppermute x5, waiting for transfers between devices: 11.8 us -> 7.98 us  [exchange(): return lax.ppermute(value, 'ctx', [(i, i ^ offset) for i in range(count)])]
    ppermute x12, starting transfers between devices: 11 us -> 14.1 us  [hop(): return lax.ppermute(value, ('dp', 'pipe', 'ctx'), route)]
    ppermute x5, starting transfers between devices: 6.77 us -> 8.13 us  [exchange(): return lax.ppermute(value, 'ctx', [(i, i ^ offset) for i in range(count)])]
  transfers between devices with their start and end apart: 21 -> 21, of which waited for: 15 -> 14; matrix products, arithmetic and copies ran while one was open for 0% -> 0% of each run, Pallas kernels for 6% -> 6%
where the time goes in v1:
time: 58.3 us; the launch traced here: 58.2 us
  starting transfers between devices  28.4 us (49%)
  waiting for transfers between devices  23.1 us (40%)
  Pallas kernels  4.74 us (8%)
  other arithmetic  1.75 us (3%)
    ppermute x12, starting transfers between devices, hop(): return lax.ppermute(value, ('dp', 'pipe', 'ctx'), route)  14.1 us
    ppermute x12, waiting for transfers between devices, hop(): return lax.ppermute(value, ('dp', 'pipe', 'ctx'), route)  10.4 us
    ppermute x5, starting transfers between devices, exchange(): return lax.ppermute(value, 'ctx', [(i, i ^ offset) for i in range(count)])  8.13 us
    ppermute x5, waiting for transfers between devices, exchange(): return lax.ppermute(value, 'ctx', [(i, i ^ offset) for i in range(count)])  7.98 us
    ppermute x3, starting transfers between devices, onward(): lax.ppermute(value, 'ctx', [(i, (i + step) % count) for i in range(count)])  6.11 us
    pallas_call x22, Pallas kernels, call(): pl.pallas_call(run, out_shape=[*outs, *(jax.ShapeDtypeStruct(a.shape, a.d...  4.74 us
    ppermute x3, waiting for transfers between devices, onward(): lax.ppermute(value, 'ctx', [(i, (i + step) % count) for i in range(count)])  3.66 us
  transfers between devices with their start and end apart: 21, of which 14 were waited for; matrix products, arithmetic and copies ran while one was open for 0% of the time, Pallas kernels for 6%

profile of v1, /device:TPU:0, one launch (start us, length us, event | category | flops | bytes accessed | tf_op | source)
XLA Modules:
  0.0 58.2 jit_solution(616098836635962068)
XLA Ops:
  0.0 1.0 %broadcast_select_fusion.refs_0_ = bf16[2,64,768]{2,1,0:T(8,128)(2,1)S(1)} fusion(bf16[2,64,768]{2,1,0:T(8,128)(2,1)} %param.5, bf16[2,64,768]{2,1,0:T(8,128)(2,1)} %param.4, pred[]{:T(512)S(6)} %eq.3), kind=kLoop, calls=%fused_computation.1 | loop fusion | flops 98304 | bytes 589825 | tf_op jit(solution)/shard_map/jit(_where)/select_n | solution.py:475
  1.2 3.1 %collective-permute-start = (bf16[32,768]{1,0:T(8,128)(2,1)S(1)}, bf16[32,768]{1,0:T(8,128)(2,1)S(1)}, u32[]{:S(2)}, u32[]{:S(2)}) collective-permute-start(bf16[32,768]{1,0:T(8,128)(2,1)S(1)} %get-tuple-element.45), channel_id=1, source_target_pairs={{0,1},{1,2},{2,3},{3,0},{4,5},{5,6},{6,7},{7,4},{8,9},{9,10},{10,1... | collective-permute-start | bytes 147464 | tf_op jit(solution)/shard_map/ppermute | solution.py:470
  4.3 2.1 %collective-permute-start.1 = (bf16[32,768]{1,0:T(8,128)(2,1)S(1)}, bf16[32,768]{1,0:T(8,128)(2,1)S(1)}, u32[]{:S(2)}, u32[]{:S(2)}) collective-permute-start(bf16[32,768]{1,0:T(8,128)(2,1)S(1)} %get-tuple-element.46), channel_id=1, source_target_pairs={{0,3},{1,0},{2,1},{3,2},{4,7},{5,4},{6,5},{7,6},{8,11},{9,8},{10,9... | collective-permute-start | bytes 147464 | tf_op jit(solution)/shard_map/ppermute | solution.py:470
  6.4 0.9 %collective-permute-start.2 = (bf16[32,768]{1,0:T(8,128)(2,1)S(1)}, bf16[32,768]{1,0:T(8,128)(2,1)S(1)}, u32[]{:S(2)}, u32[]{:S(2)}) collective-permute-start(bf16[32,768]{1,0:T(8,128)(2,1)S(1)} %get-tuple-element.47), channel_id=1, source_target_pairs={{0,2},{1,3},{2,0},{3,1},{4,6},{5,7},{6,4},{7,5},{8,10},{9,11},{10,... | collective-permute-start | bytes 147464 | tf_op jit(solution)/shard_map/ppermute | solution.py:470
  7.3 0.5 hold.1
  7.8 0.7 %collective-permute-done.refs_0_ = bf16[32,768]{1,0:T(8,128)(2,1)S(1)} collective-permute-done((bf16[32,768]{1,0:T(8,128)(2,1)S(1)}, bf16[32,768]{1,0:T(8,128)(2,1)S(1)}, u32[]{:S(2)}, u32[]{:S(2)}) %collective-permute-start) | collective-permute-done | bytes 49184 | tf_op jit(solution)/shard_map/ppermute | solution.py:470
  8.9 2.6 %collective-permute-done.2.refs_2_ = bf16[32,768]{1,0:T(8,128)(2,1)S(1)} collective-permute-done((bf16[32,768]{1,0:T(8,128)(2,1)S(1)}, bf16[32,768]{1,0:T(8,128)(2,1)S(1)}, u32[]{:S(2)}, u32[]{:S(2)}) %collective-permute-start.2) | collective-permute-done | bytes 49184 | tf_op jit(solution)/shard_map/ppermute | solution.py:470
  11.5 0.6 %first.1 = (bf16[128,768]{1,0:T(8,128)(2,1)S(1)}, bf16[64,768]{1,0:T(8,128)(2,1)S(1)}, f32[64,384]{1,0:T(8,128)S(1)}) custom-call(bf16[32,768]{1,0:T(8,128)(2,1)S(1)} %collective-permute-done.refs_0_, bf16[32,768]{1,0:T(8,128)(2,1)S(1)} %collective-permute-done.1.refs_1_, bf16[32,768]{1,0:T(8,128)(2,1)S(1)} %collective-permute-done.2.refs_2_, ...), custom_call_target="tpu_custom_call" | custom-call | flops 150994944 | bytes 2949120 | tf_op jit(solution)/shard_map/first/pallas_call | solution.py:421
  12.2 0.7 %collective-permute-start.3 = (bf16[64,768]{1,0:T(8,128)(2,1)S(1)}, bf16[64,768]{1,0:T(8,128)(2,1)S(1)}, u32[]{:S(2)}, u32[]{:S(2)}) collective-permute-start(bf16[64,768]{1,0:T(8,128)(2,1)S(1)} %get-tuple-element.52.refs_3_), channel_id=1, source_target_pairs={{0,4},{1,5},{2,6},{3,7},{4,0},{5,1},{6,2},{7,3},{8,24},{9,25},{10,... | collective-permute-start | bytes 294920 | tf_op jit(solution)/shard_map/ppermute | solution.py:467
  12.8 0.6 %fore.5 = (bf16[64,768]{1,0:T(8,128)(2,1)S(1)}, f32[64,384]{1,0:T(8,128)S(1)}) custom-call(bf16[128,768]{1,0:T(8,128)(2,1)S(1)} %get-tuple-element.51.refs_0_.refs_1_, bf16[1,3,768,384]{3,2,1,0:T(8,128)(2,1)S(1)} %get-tuple-element.49.refs_4_.refs_1_.refs_0_.refs_2_, bf16[1,384,768]{2,1,0:T(8,128)(2,1)S(1)} %get-tuple-element.50.refs_5_.refs_2_.refs_1_, ...), custom_call_target="tpu_custom_call" | custom-call | flops 150994944 | bytes 2752512 | tf_op jit(solution)/shard_map/fore/pallas_call | solution.py:421
  13.4 0.8 %collective-permute-start.4 = (bf16[64,768]{1,0:T(8,128)(2,1)S(1)}, bf16[64,768]{1,0:T(8,128)(2,1)S(1)}, u32[]{:S(2)}, u32[]{:S(2)}) collective-permute-start(bf16[64,768]{1,0:T(8,128)(2,1)S(1)} %get-tuple-element.53.refs_4_), channel_id=1, source_target_pairs={{0,4},{1,5},{2,6},{3,7},{4,0},{5,1},{6,2},{7,3},{8,24},{9,25},{10,... | collective-permute-start | bytes 294920 | tf_op jit(solution)/shard_map/ppermute | solution.py:467
  14.3 2.9 %collective-permute-done.3.refs_0_.refs_2_.refs_1_ = bf16[64,768]{1,0:T(8,128)(2,1)S(1)} collective-permute-done((bf16[64,768]{1,0:T(8,128)(2,1)S(1)}, bf16[64,768]{1,0:T(8,128)(2,1)S(1)}, u32[]{:S(2)}, u32[]{:S(2)}) %collective-permute-start.3) | collective-permute-done | bytes 98336 | tf_op jit(solution)/shard_map/ppermute | solution.py:467
  17.2 2.1 %collective-permute-done.4.refs_0_.refs_3_.refs_2_ = bf16[64,768]{1,0:T(8,128)(2,1)S(1)} collective-permute-done((bf16[64,768]{1,0:T(8,128)(2,1)S(1)}, bf16[64,768]{1,0:T(8,128)(2,1)S(1)}, u32[]{:S(2)}, u32[]{:S(2)}) %collective-permute-start.4) | collective-permute-done | bytes 98336 | tf_op jit(solution)/shard_map/ppermute | solution.py:467
  19.3 0.7 %transpose.1 = (bf16[1,3,384,768]{3,2,1,0:T(8,128)(2,1)S(1)}, bf16[1,768,384]{2,1,0:T(8,128)(2,1)S(1)}) custom-call(bf16[1,3,768,384]{3,2,1,0:T(8,128)(2,1)S(1)} %get-tuple-element.49.refs_4_.refs_1_.refs_0_.refs_2_, bf16[1,384,768]{2,1,0:T(8,128)(2,1)S(1)} %get-tuple-element.50.refs_5_.refs_2_.refs_1_, ...), custom_call_target="tpu_custom_call" | custom-call | bytes 4718592 | tf_op jit(solution)/shard_map/transpose/pallas_call | solution.py:421
  20.0 3.2 %collective-permute-start.7 = (bf16[64,768]{1,0:T(8,128)(2,1)S(1)}, bf16[64,768]{1,0:T(8,128)(2,1)S(1)}, u32[]{:S(2)}, u32[]{:S(2)}) collective-permute-start(bf16[64,768]{1,0:T(8,128)(2,1)S(1)} %get-tuple-element.58.refs_3_.refs_12_.refs_5_), channel_id=1, source_target_pairs={{0,8},{1,9},{2,10},{3,11},{4,20},{5,21},{6,22},{7,23},{8,12},{9,13... | collective-permute-start | bytes 294920 | tf_op jit(solution)/shard_map/ppermute | solution.py:467
  23.2 1.1 %collective-permute-start.8 = (bf16[64,768]{1,0:T(8,128)(2,1)S(1)}, bf16[64,768]{1,0:T(8,128)(2,1)S(1)}, u32[]{:S(2)}, u32[]{:S(2)}) collective-permute-start(bf16[64,768]{1,0:T(8,128)(2,1)S(1)} %get-tuple-element.59.refs_13_.refs_6_), channel_id=1, source_target_pairs={{0,8},{1,9},{2,10},{3,11},{4,20},{5,21},{6,22},{7,23},{8,12},{9,13... | collective-permute-start | bytes 294920 | tf_op jit(solution)/shard_map/ppermute | solution.py:467
  24.6 1.9 %collective-permute-done.7.refs_0_.refs_5_ = bf16[64,768]{1,0:T(8,128)(2,1)S(1)} collective-permute-done((bf16[64,768]{1,0:T(8,128)(2,1)S(1)}, bf16[64,768]{1,0:T(8,128)(2,1)S(1)}, u32[]{:S(2)}, u32[]{:S(2)}) %collective-permute-start.7) | collective-permute-done | bytes 98336 | tf_op jit(solution)/shard_map/ppermute | solution.py:467
  26.5 2.9 %collective-permute-done.8.refs_0_.refs_6_ = bf16[64,768]{1,0:T(8,128)(2,1)S(1)} collective-permute-done((bf16[64,768]{1,0:T(8,128)(2,1)S(1)}, bf16[64,768]{1,0:T(8,128)(2,1)S(1)}, u32[]{:S(2)}, u32[]{:S(2)}) %collective-permute-start.8) | collective-permute-done | bytes 98336 | tf_op jit(solution)/shard_map/ppermute | solution.py:467
  29.5 0.6 columns.1
  30.4 2.9 %collective-permute-start.14 = (bf16[64,768]{1,0:T(8,128)(2,1)S(1)}, bf16[64,768]{1,0:T(8,128)(2,1)S(1)}, u32[]{:S(2)}, u32[]{:S(2)}) collective-permute-start(bf16[64,768]{1,0:T(8,128)(2,1)S(1)} %get-tuple-element.75.refs_5_.refs_2_), channel_id=1, source_target_pairs={{0,8},{1,9},{2,10},{3,11},{4,0},{5,1},{6,2},{7,3},{8,4},{9,5},{10,... | collective-permute-start | bytes 294920 | tf_op jit(solution)/shard_map/ppermute | solution.py:467
  33.3 1.9 %collective-permute-start.13 = (bf16[64,768]{1,0:T(8,128)(2,1)S(1)}, bf16[64,768]{1,0:T(8,128)(2,1)S(1)}, u32[]{:S(2)}, u32[]{:S(2)}) collective-permute-start(bf16[64,768]{1,0:T(8,128)(2,1)S(1)} %get-tuple-element.76.refs_3_.refs_6_), channel_id=1, source_target_pairs={{0,8},{1,9},{2,10},{3,11},{4,0},{5,1},{6,2},{7,3},{8,4},{9,5},{10,... | collective-permute-start | bytes 294920 | tf_op jit(solution)/shard_map/ppermute | solution.py:467
  35.3 2.4 %collective-permute-start.12 = (bf16[384,128]{1,0:T(8,128)(2,1)S(1)}, bf16[384,128]{1,0:T(8,128)(2,1)S(1)}, u32[]{:S(2)}, u32[]{:S(2)}) collective-permute-start(bf16[384,128]{1,0:T(8,128)(2,1)S(1)} %message.1.refs_7_), channel_id=1, source_target_pairs={{0,2},{1,3},{2,0},{3,1},{4,6},{5,7},{6,4},{7,5},{8,10},{9,11},{10,... | collective-permute-start | bytes 294920 | tf_op jit(solution)/shard_map/ppermute | solution.py:473
  37.8 0.6 %collective-permute-start.16 = (bf16[64,768]{1,0:T(8,128)(2,1)S(1)}, bf16[64,768]{1,0:T(8,128)(2,1)S(1)}, u32[]{:S(2)}, u32[]{:S(2)}) collective-permute-start(bf16[64,768]{1,0:T(8,128)(2,1)S(1)} %get-tuple-element.77.refs_5_.refs_6_), channel_id=1, source_target_pairs={{0,12},{1,13},{2,14},{3,15},{4,0},{5,1},{6,2},{7,3},{8,24},{9,25},... | collective-permute-start | bytes 294920 | tf_op jit(solution)/shard_map/ppermute | solution.py:467
  38.4 2.9 %collective-permute-start.15 = (bf16[64,768]{1,0:T(8,128)(2,1)S(1)}, bf16[64,768]{1,0:T(8,128)(2,1)S(1)}, u32[]{:S(2)}, u32[]{:S(2)}) collective-permute-start(bf16[64,768]{1,0:T(8,128)(2,1)S(1)} %get-tuple-element.78.refs_7_), channel_id=1, source_target_pairs={{0,12},{1,13},{2,14},{3,15},{4,0},{5,1},{6,2},{7,3},{8,24},{9,25},... | collective-permute-start | bytes 294920 | tf_op jit(solution)/shard_map/ppermute | solution.py:467
  41.2 1.5 %collective-permute-done.12.refs_8_.refs_1_.refs_3_ = bf16[384,128]{1,0:T(8,128)(2,1)S(1)} collective-permute-done((bf16[384,128]{1,0:T(8,128)(2,1)S(1)}, bf16[384,128]{1,0:T(8,128)(2,1)S(1)}, u32[]{:S(2)}, u32[]{:S(2)}) %collective-permute-start.12) | collective-permute-done | bytes 98336 | tf_op jit(solution)/shard_map/ppermute | solution.py:473
  43.7 3.9 %collective-permute-start.17 = (bf16[128,384]{1,0:T(8,128)(2,1)S(1)}, bf16[128,384]{1,0:T(8,128)(2,1)S(1)}, u32[]{:S(2)}, u32[]{:S(2)}) collective-permute-start(bf16[128,384]{1,0:T(8,128)(2,1)S(1)} %head.3.refs_4_), channel_id=1, source_target_pairs={{0,2},{1,3},{2,0},{3,1},{4,6},{5,7},{6,4},{7,5},{8,10},{9,11},{10,... | collective-permute-start | bytes 294920 | tf_op jit(solution)/shard_map/ppermute | solution.py:473
  47.5 3.3 %collective-permute-done.17.refs_5_ = bf16[128,384]{1,0:T(8,128)(2,1)S(1)} collective-permute-done((bf16[128,384]{1,0:T(8,128)(2,1)S(1)}, bf16[128,384]{1,0:T(8,128)(2,1)S(1)}, u32[]{:S(2)}, u32[]{:S(2)}) %collective-permute-start.17) | collective-permute-done | bytes 98336 | tf_op jit(solution)/shard_map/ppermute | solution.py:473
  50.8 1.5 %collective-permute-start.19 = (bf16[128,384]{1,0:T(8,128)(2,1)S(1)}, bf16[128,384]{1,0:T(8,128)(2,1)S(1)}, u32[]{:S(2)}, u32[]{:S(2)}) collective-permute-start(bf16[128,384]{1,0:T(8,128)(2,1)S(1)} %collective-permute-done.17.refs_5_), channel_id=1, source_target_pairs={{0,1},{1,0},{2,3},{3,2},{4,5},{5,4},{6,7},{7,6},{8,9},{9,8},{10,11... | collective-permute-start | bytes 294920 | tf_op jit(solution)/shard_map/ppermute | solution.py:473
  52.3 0.6 collective-permute-done.18.refs_6_
  52.9 2.6 %collective-permute-done.19.refs_7_ = bf16[128,384]{1,0:T(8,128)(2,1)S(1)} collective-permute-done((bf16[128,384]{1,0:T(8,128)(2,1)S(1)}, bf16[128,384]{1,0:T(8,128)(2,1)S(1)}, u32[]{:S(2)}, u32[]{:S(2)}) %collective-permute-start.19) | collective-permute-done | bytes 98336 | tf_op jit(solution)/shard_map/ppermute | solution.py:473
  56.3 1.1 %collective-permute-done.20 = bf16[3,96,384]{2,1,0:T(8,128)(2,1)S(1)} collective-permute-done((bf16[3,96,384]{2,1,0:T(8,128)(2,1)S(1)}, bf16[3,96,384]{2,1,0:T(8,128)(2,1)S(1)}, u32[]{:S(2)}, u32[]{:S(2)}) %collective-permute-start.20) | collective-permute-done | bytes 221216 | tf_op jit(solution)/shard_map/ppermute | solution.py:633
  57.4 0.8 %add_bitcast_fusion = f32[1,3,96,384]{3,2,1,0:T(8,128)} fusion(f32[3,96,384]{2,1,0:T(8,128)S(1)} %grad.3, bf16[3,96,384]{2,1,0:T(8,128)(2,1)S(1)} %collective-permute-done.20), kind=kLoop, calls=%fused_computation | loop fusion | flops 221184 | bytes 1105920 | tf_op jit(solution)/shard_map/broadcast_in_dim | solution.py:634
  (38 shorter events, 3.2 us)
Async XLA Ops:
  1.0 6.4 %copy-start = (bf16[1,3,768,384]{3,2,1,0:T(8,128)(2,1)S(1)}, bf16[1,3,768,384]{3,2,1,0:T(8,128)(2,1)}, u32[]{:S(2)}) copy-start(bf16[1,3,768,384]{3,2,1,0:T(8,128)(2,1)} %refs_0_.1) | copy-start | bytes 5308420
  1.0 6.4 %copy-start.1 = (bf16[1,384,768]{2,1,0:T(8,128)(2,1)S(1)}, bf16[1,384,768]{2,1,0:T(8,128)(2,1)}, u32[]{:S(2)}) copy-start(bf16[1,384,768]{2,1,0:T(8,128)(2,1)} %refs_1_.1) | copy-start | bytes 1769476
  1.2 7.3 %collective-permute-start = (bf16[32,768]{1,0:T(8,128)(2,1)S(1)}, bf16[32,768]{1,0:T(8,128)(2,1)S(1)}, u32[]{:S(2)}, u32[]{:S(2)}) collective-permute-start(bf16[32,768]{1,0:T(8,128)(2,1)S(1)} %get-tuple-element.45), channel_id=1, source_target_pairs={{0,1},{1,2},{2,3},{3,0},{4,5},{5,6},{6,7},{7,4},{8,9},{9,10},{10,1... | collective-permute-start | bytes 147464 | tf_op jit(solution)/shard_map/ppermute | solution.py:470
  4.3 4.6 %collective-permute-start.1 = (bf16[32,768]{1,0:T(8,128)(2,1)S(1)}, bf16[32,768]{1,0:T(8,128)(2,1)S(1)}, u32[]{:S(2)}, u32[]{:S(2)}) collective-permute-start(bf16[32,768]{1,0:T(8,128)(2,1)S(1)} %get-tuple-element.46), channel_id=1, source_target_pairs={{0,3},{1,0},{2,1},{3,2},{4,7},{5,4},{6,5},{7,6},{8,11},{9,8},{10,9... | collective-permute-start | bytes 147464 | tf_op jit(solution)/shard_map/ppermute | solution.py:470
  6.4 5.1 %collective-permute-start.2 = (bf16[32,768]{1,0:T(8,128)(2,1)S(1)}, bf16[32,768]{1,0:T(8,128)(2,1)S(1)}, u32[]{:S(2)}, u32[]{:S(2)}) collective-permute-start(bf16[32,768]{1,0:T(8,128)(2,1)S(1)} %get-tuple-element.47), channel_id=1, source_target_pairs={{0,2},{1,3},{2,0},{3,1},{4,6},{5,7},{6,4},{7,5},{8,10},{9,11},{10,... | collective-permute-start | bytes 147464 | tf_op jit(solution)/shard_map/ppermute | solution.py:470
  12.2 5.0 %collective-permute-start.3 = (bf16[64,768]{1,0:T(8,128)(2,1)S(1)}, bf16[64,768]{1,0:T(8,128)(2,1)S(1)}, u32[]{:S(2)}, u32[]{:S(2)}) collective-permute-start(bf16[64,768]{1,0:T(8,128)(2,1)S(1)} %get-tuple-element.52.refs_3_), channel_id=1, source_target_pairs={{0,4},{1,5},{2,6},{3,7},{4,0},{5,1},{6,2},{7,3},{8,24},{9,25},{10,... | collective-permute-start | bytes 294920 | tf_op jit(solution)/shard_map/ppermute | solution.py:467
  13.4 5.8 %collective-permute-start.4 = (bf16[64,768]{1,0:T(8,128)(2,1)S(1)}, bf16[64,768]{1,0:T(8,128)(2,1)S(1)}, u32[]{:S(2)}, u32[]{:S(2)}) collective-permute-start(bf16[64,768]{1,0:T(8,128)(2,1)S(1)} %get-tuple-element.53.refs_4_), channel_id=1, source_target_pairs={{0,4},{1,5},{2,6},{3,7},{4,0},{5,1},{6,2},{7,3},{8,24},{9,25},{10,... | collective-permute-start | bytes 294920 | tf_op jit(solution)/shard_map/ppermute | solution.py:467
  17.1 2.8 %collective-permute-start.5 = (bf16[64,768]{1,0:T(8,128)(2,1)S(1)}, bf16[64,768]{1,0:T(8,128)(2,1)S(1)}, u32[]{:S(2)}, u32[]{:S(2)}) collective-permute-start(bf16[64,768]{1,0:T(8,128)(2,1)S(1)} %get-tuple-element.54.refs_3_.refs_2_), channel_id=1, source_target_pairs={{0,16},{1,17},{2,18},{3,19},{4,8},{5,9},{6,10},{7,11},{8,12},{9,13... | collective-permute-start | bytes 294920 | tf_op jit(solution)/shard_map/ppermute | solution.py:467
  19.3 3.9 %collective-permute-start.6 = (bf16[64,768]{1,0:T(8,128)(2,1)S(1)}, bf16[64,768]{1,0:T(8,128)(2,1)S(1)}, u32[]{:S(2)}, u32[]{:S(2)}) collective-permute-start(bf16[64,768]{1,0:T(8,128)(2,1)S(1)} %get-tuple-element.55.refs_3_.refs_4_), channel_id=1, source_target_pairs={{0,16},{1,17},{2,18},{3,19},{4,8},{5,9},{6,10},{7,11},{8,12},{9,13... | collective-permute-start | bytes 294920 | tf_op jit(solution)/shard_map/ppermute | solution.py:467
  20.0 6.5 %collective-permute-start.7 = (bf16[64,768]{1,0:T(8,128)(2,1)S(1)}, bf16[64,768]{1,0:T(8,128)(2,1)S(1)}, u32[]{:S(2)}, u32[]{:S(2)}) collective-permute-start(bf16[64,768]{1,0:T(8,128)(2,1)S(1)} %get-tuple-element.58.refs_3_.refs_12_.refs_5_), channel_id=1, source_target_pairs={{0,8},{1,9},{2,10},{3,11},{4,20},{5,21},{6,22},{7,23},{8,12},{9,13... | collective-permute-start | bytes 294920 | tf_op jit(solution)/shard_map/ppermute | solution.py:467
  23.2 6.3 %collective-permute-start.8 = (bf16[64,768]{1,0:T(8,128)(2,1)S(1)}, bf16[64,768]{1,0:T(8,128)(2,1)S(1)}, u32[]{:S(2)}, u32[]{:S(2)}) collective-permute-start(bf16[64,768]{1,0:T(8,128)(2,1)S(1)} %get-tuple-element.59.refs_13_.refs_6_), channel_id=1, source_target_pairs={{0,8},{1,9},{2,10},{3,11},{4,20},{5,21},{6,22},{7,23},{8,12},{9,13... | collective-permute-start | bytes 294920 | tf_op jit(solution)/shard_map/ppermute | solution.py:467
  26.5 3.9 %collective-permute-start.10 = (bf16[64,768]{1,0:T(8,128)(2,1)S(1)}, bf16[64,768]{1,0:T(8,128)(2,1)S(1)}, u32[]{:S(2)}, u32[]{:S(2)}) collective-permute-start(bf16[64,768]{1,0:T(8,128)(2,1)S(1)} %get-tuple-element.70.refs_5_.refs_7_), channel_id=1, source_target_pairs={{0,16},{1,17},{2,18},{3,19},{4,20},{5,21},{6,22},{7,23},{8,12},{9,... | collective-permute-start | bytes 294920 | tf_op jit(solution)/shard_map/ppermute | solution.py:467
  29.5 3.9 %collective-permute-start.11 = (bf16[64,768]{1,0:T(8,128)(2,1)S(1)}, bf16[64,768]{1,0:T(8,128)(2,1)S(1)}, u32[]{:S(2)}, u32[]{:S(2)}) collective-permute-start(bf16[64,768]{1,0:T(8,128)(2,1)S(1)} %get-tuple-element.71.refs_8_), channel_id=1, source_target_pairs={{0,16},{1,17},{2,18},{3,19},{4,20},{5,21},{6,22},{7,23},{8,12},{9,... | collective-permute-start | bytes 294920 | tf_op jit(solution)/shard_map/ppermute | solution.py:467
  30.0 5.3 %collective-permute-start.9 = (bf16[384,128]{1,0:T(8,128)(2,1)S(1)}, bf16[384,128]{1,0:T(8,128)(2,1)S(1)}, u32[]{:S(2)}, u32[]{:S(2)}) collective-permute-start(bf16[384,128]{1,0:T(8,128)(2,1)S(1)} %get-tuple-element.74), channel_id=1, source_target_pairs={{0,1},{1,0},{2,3},{3,2},{4,5},{5,4},{6,7},{7,6},{8,9},{9,8},{10,11... | collective-permute-start | bytes 294920 | tf_op jit(solution)/shard_map/ppermute | solution.py:473
  30.4 7.4 %collective-permute-start.14 = (bf16[64,768]{1,0:T(8,128)(2,1)S(1)}, bf16[64,768]{1,0:T(8,128)(2,1)S(1)}, u32[]{:S(2)}, u32[]{:S(2)}) collective-permute-start(bf16[64,768]{1,0:T(8,128)(2,1)S(1)} %get-tuple-element.75.refs_5_.refs_2_), channel_id=1, source_target_pairs={{0,8},{1,9},{2,10},{3,11},{4,0},{5,1},{6,2},{7,3},{8,4},{9,5},{10,... | collective-permute-start | bytes 294920 | tf_op jit(solution)/shard_map/ppermute | solution.py:467
  33.3 5.1 %collective-permute-start.13 = (bf16[64,768]{1,0:T(8,128)(2,1)S(1)}, bf16[64,768]{1,0:T(8,128)(2,1)S(1)}, u32[]{:S(2)}, u32[]{:S(2)}) collective-permute-start(bf16[64,768]{1,0:T(8,128)(2,1)S(1)} %get-tuple-element.76.refs_3_.refs_6_), channel_id=1, source_target_pairs={{0,8},{1,9},{2,10},{3,11},{4,0},{5,1},{6,2},{7,3},{8,4},{9,5},{10,... | collective-permute-start | bytes 294920 | tf_op jit(solution)/shard_map/ppermute | solution.py:467
  35.3 7.4 %collective-permute-start.12 = (bf16[384,128]{1,0:T(8,128)(2,1)S(1)}, bf16[384,128]{1,0:T(8,128)(2,1)S(1)}, u32[]{:S(2)}, u32[]{:S(2)}) collective-permute-start(bf16[384,128]{1,0:T(8,128)(2,1)S(1)} %message.1.refs_7_), channel_id=1, source_target_pairs={{0,2},{1,3},{2,0},{3,1},{4,6},{5,7},{6,4},{7,5},{8,10},{9,11},{10,... | collective-permute-start | bytes 294920 | tf_op jit(solution)/shard_map/ppermute | solution.py:473
  37.8 5.0 %collective-permute-start.16 = (bf16[64,768]{1,0:T(8,128)(2,1)S(1)}, bf16[64,768]{1,0:T(8,128)(2,1)S(1)}, u32[]{:S(2)}, u32[]{:S(2)}) collective-permute-start(bf16[64,768]{1,0:T(8,128)(2,1)S(1)} %get-tuple-element.77.refs_5_.refs_6_), channel_id=1, source_target_pairs={{0,12},{1,13},{2,14},{3,15},{4,0},{5,1},{6,2},{7,3},{8,24},{9,25},... | collective-permute-start | bytes 294920 | tf_op jit(solution)/shard_map/ppermute | solution.py:467
  38.4 5.1 %collective-permute-start.15 = (bf16[64,768]{1,0:T(8,128)(2,1)S(1)}, bf16[64,768]{1,0:T(8,128)(2,1)S(1)}, u32[]{:S(2)}, u32[]{:S(2)}) collective-permute-start(bf16[64,768]{1,0:T(8,128)(2,1)S(1)} %get-tuple-element.78.refs_7_), channel_id=1, source_target_pairs={{0,12},{1,13},{2,14},{3,15},{4,0},{5,1},{6,2},{7,3},{8,24},{9,25},... | collective-permute-start | bytes 294920 | tf_op jit(solution)/shard_map/ppermute | solution.py:467
  43.7 7.2 %collective-permute-start.17 = (bf16[128,384]{1,0:T(8,128)(2,1)S(1)}, bf16[128,384]{1,0:T(8,128)(2,1)S(1)}, u32[]{:S(2)}, u32[]{:S(2)}) collective-permute-start(bf16[128,384]{1,0:T(8,128)(2,1)S(1)} %head.3.refs_4_), channel_id=1, source_target_pairs={{0,2},{1,3},{2,0},{3,1},{4,6},{5,7},{6,4},{7,5},{8,10},{9,11},{10,... | collective-permute-start | bytes 294920 | tf_op jit(solution)/shard_map/ppermute | solution.py:473
  47.5 5.3 %collective-permute-start.18 = (bf16[128,384]{1,0:T(8,128)(2,1)S(1)}, bf16[128,384]{1,0:T(8,128)(2,1)S(1)}, u32[]{:S(2)}, u32[]{:S(2)}) collective-permute-start(bf16[128,384]{1,0:T(8,128)(2,1)S(1)} %head.3.refs_4_), channel_id=1, source_target_pairs={{0,1},{1,0},{2,3},{3,2},{4,5},{5,4},{6,7},{7,6},{8,9},{9,8},{10,11... | collective-permute-start | bytes 294920 | tf_op jit(solution)/shard_map/ppermute | solution.py:473
  50.8 4.6 %collective-permute-start.19 = (bf16[128,384]{1,0:T(8,128)(2,1)S(1)}, bf16[128,384]{1,0:T(8,128)(2,1)S(1)}, u32[]{:S(2)}, u32[]{:S(2)}) collective-permute-start(bf16[128,384]{1,0:T(8,128)(2,1)S(1)} %collective-permute-done.17.refs_5_), channel_id=1, source_target_pairs={{0,1},{1,0},{2,3},{3,2},{4,5},{5,4},{6,7},{7,6},{8,9},{9,8},{10,11... | collective-permute-start | bytes 294920 | tf_op jit(solution)/shard_map/ppermute | solution.py:473
  55.8 1.5 %collective-permute-start.20 = (bf16[3,96,384]{2,1,0:T(8,128)(2,1)S(1)}, bf16[3,96,384]{2,1,0:T(8,128)(2,1)S(1)}, u32[]{:S(2)}, u32[]{:S(2)}) collective-permute-start(bf16[3,96,384]{2,1,0:T(8,128)(2,1)S(1)} %grad.2.refs_8_), channel_id=1, source_target_pairs={{0,16},{16,0},{1,17},{17,1},{2,18},{18,2},{3,19},{19,3},{4,20},{20... | collective-permute-start | bytes 663560 | tf_op jit(solution)/shard_map/ppermute | solution.py:633

commit v2 on v1

--- a/solution.py
+++ b/solution.py
@@ -503,7 +503,8 @@
     for level in range(last):
         if level > 0:
             third = last if level > 1 else None
-            xs.append([hop(out, level - 1, level, third) for out in outs])
+            xs.append([hop(out, level - 1, level, third) for out in outs[:-1]])
+            xs[level].append(hop(outs[-1], level - 1, level))
             outs = []
             pres.append([])
         for seq in range(len(outs), seq_count):
@@ -579,7 +580,9 @@
             outs.append(dy)
             dpres[level].append(dpre)
         sent = outs
-        dys = [hop(dy, level, level - 1, 0 if level > 1 else last) for dy in outs]
+        third = 0 if level > 1 else last
+        dys = [hop(dy, level, level - 1, third) for dy in outs[:-1]]
+        dys.append(hop(outs[-1], level, level - 1, None if level > 1 else last))
         bit *= 2
         moving = sorted(key for key in blocks if key[0] & bit)
         if moving:

time: 58.3 us -> 58.5 us (level)
  waiting for transfers between devices: 23.1 us -> 28.6 us
  starting transfers between devices: 28.4 us -> 23.1 us
    ppermute x5, waiting for transfers between devices: 7.98 us -> 13.8 us  [exchange(): return lax.ppermute(value, 'ctx', [(i, i ^ offset) for i in range(count)])]
    ppermute x5, starting transfers between devices: 8.13 us -> 4.85 us  [exchange(): return lax.ppermute(value, 'ctx', [(i, i ^ offset) for i in range(count)])]
    ppermute x12, starting transfers between devices: 14.1 us -> 12.1 us  [hop(): return lax.ppermute(value, ('dp', 'pipe', 'ctx'), route)]
where the time goes in v2:
time: 58.5 us; the launch traced here: 58.4 us
  waiting for transfers between devices  28.6 us (49%)
  starting transfers between devices  23.1 us (39%)
  Pallas kernels  4.74 us (8%)
  other arithmetic  1.75 us (3%)
    ppermute x5, waiting for transfers between devices, exchange(): return lax.ppermute(value, 'ctx', [(i, i ^ offset) for i in range(count)])  13.8 us
    ppermute x12, starting transfers between devices, hop(): return lax.ppermute(value, ('dp', 'pipe', 'ctx'), route)  12.1 us
    ppermute x12, waiting for transfers between devices, hop(): return lax.ppermute(value, ('dp', 'pipe', 'ctx'), route)  10.1 us
    ppermute x3, starting transfers between devices, onward(): lax.ppermute(value, 'ctx', [(i, (i + step) % count) for i in range(count)])  6.11 us
    ppermute x5, starting transfers between devices, exchange(): return lax.ppermute(value, 'ctx', [(i, i ^ offset) for i in range(count)])  4.85 us
    pallas_call x22, Pallas kernels, call(): pl.pallas_call(run, out_shape=[*outs, *(jax.ShapeDtypeStruct(a.shape, a.d...  4.74 us
    ppermute x3, waiting for transfers between devices, onward(): lax.ppermute(value, 'ctx', [(i, (i + step) % count) for i in range(count)])  3.66 us
  transfers between devices with their start and end apart: 21, of which 14 were waited for; matrix products, arithmetic and copies ran while one was open for 0% of the time, Pallas kernels for 6%

profile of v2, /device:TPU:0, one launch (start us, length us, event | category | flops | bytes accessed | tf_op | source)
XLA Modules:
  0.0 58.4 jit_solution(702076558208055504)
XLA Ops:
  0.0 1.0 %broadcast_select_fusion.refs_0_ = bf16[2,64,768]{2,1,0:T(8,128)(2,1)S(1)} fusion(bf16[2,64,768]{2,1,0:T(8,128)(2,1)} %param.5, bf16[2,64,768]{2,1,0:T(8,128)(2,1)} %param.4, pred[]{:T(512)S(6)} %eq.3), kind=kLoop, calls=%fused_computation.1 | loop fusion | flops 98304 | bytes 589825 | tf_op jit(solution)/shard_map/jit(_where)/select_n | solution.py:475
  1.2 3.1 %collective-permute-start = (bf16[32,768]{1,0:T(8,128)(2,1)S(1)}, bf16[32,768]{1,0:T(8,128)(2,1)S(1)}, u32[]{:S(2)}, u32[]{:S(2)}) collective-permute-start(bf16[32,768]{1,0:T(8,128)(2,1)S(1)} %get-tuple-element.45), channel_id=1, source_target_pairs={{0,1},{1,2},{2,3},{3,0},{4,5},{5,6},{6,7},{7,4},{8,9},{9,10},{10,1... | collective-permute-start | bytes 147464 | tf_op jit(solution)/shard_map/ppermute | solution.py:470
  4.3 2.1 %collective-permute-start.1 = (bf16[32,768]{1,0:T(8,128)(2,1)S(1)}, bf16[32,768]{1,0:T(8,128)(2,1)S(1)}, u32[]{:S(2)}, u32[]{:S(2)}) collective-permute-start(bf16[32,768]{1,0:T(8,128)(2,1)S(1)} %get-tuple-element.46), channel_id=1, source_target_pairs={{0,3},{1,0},{2,1},{3,2},{4,7},{5,4},{6,5},{7,6},{8,11},{9,8},{10,9... | collective-permute-start | bytes 147464 | tf_op jit(solution)/shard_map/ppermute | solution.py:470
  6.4 0.9 %collective-permute-start.2 = (bf16[32,768]{1,0:T(8,128)(2,1)S(1)}, bf16[32,768]{1,0:T(8,128)(2,1)S(1)}, u32[]{:S(2)}, u32[]{:S(2)}) collective-permute-start(bf16[32,768]{1,0:T(8,128)(2,1)S(1)} %get-tuple-element.47), channel_id=1, source_target_pairs={{0,2},{1,3},{2,0},{3,1},{4,6},{5,7},{6,4},{7,5},{8,10},{9,11},{10,... | collective-permute-start | bytes 147464 | tf_op jit(solution)/shard_map/ppermute | solution.py:470
  7.3 0.5 hold.1
  7.8 0.7 %collective-permute-done.refs_0_ = bf16[32,768]{1,0:T(8,128)(2,1)S(1)} collective-permute-done((bf16[32,768]{1,0:T(8,128)(2,1)S(1)}, bf16[32,768]{1,0:T(8,128)(2,1)S(1)}, u32[]{:S(2)}, u32[]{:S(2)}) %collective-permute-start) | collective-permute-done | bytes 49184 | tf_op jit(solution)/shard_map/ppermute | solution.py:470
  8.5 0.4 collective-permute-done.1.refs_1_
  8.9 2.6 %collective-permute-done.2.refs_2_ = bf16[32,768]{1,0:T(8,128)(2,1)S(1)} collective-permute-done((bf16[32,768]{1,0:T(8,128)(2,1)S(1)}, bf16[32,768]{1,0:T(8,128)(2,1)S(1)}, u32[]{:S(2)}, u32[]{:S(2)}) %collective-permute-start.2) | collective-permute-done | bytes 49184 | tf_op jit(solution)/shard_map/ppermute | solution.py:470
  11.5 0.6 %first.1 = (bf16[128,768]{1,0:T(8,128)(2,1)S(1)}, bf16[64,768]{1,0:T(8,128)(2,1)S(1)}, f32[64,384]{1,0:T(8,128)S(1)}) custom-call(bf16[32,768]{1,0:T(8,128)(2,1)S(1)} %collective-permute-done.refs_0_, bf16[32,768]{1,0:T(8,128)(2,1)S(1)} %collective-permute-done.1.refs_1_, bf16[32,768]{1,0:T(8,128)(2,1)S(1)} %collective-permute-done.2.refs_2_, ...), custom_call_target="tpu_custom_call" | custom-call | flops 150994944 | bytes 2949120 | tf_op jit(solution)/shard_map/first/pallas_call | solution.py:421
  12.2 0.7 %collective-permute-start.3 = (bf16[64,768]{1,0:T(8,128)(2,1)S(1)}, bf16[64,768]{1,0:T(8,128)(2,1)S(1)}, u32[]{:S(2)}, u32[]{:S(2)}) collective-permute-start(bf16[64,768]{1,0:T(8,128)(2,1)S(1)} %get-tuple-element.52.refs_3_), channel_id=1, source_target_pairs={{0,4},{1,5},{2,6},{3,7},{4,0},{5,1},{6,2},{7,3},{8,24},{9,25},{10,... | collective-permute-start | bytes 294920 | tf_op jit(solution)/shard_map/ppermute | solution.py:467
  12.8 0.6 %fore.5 = (bf16[64,768]{1,0:T(8,128)(2,1)S(1)}, f32[64,384]{1,0:T(8,128)S(1)}) custom-call(bf16[128,768]{1,0:T(8,128)(2,1)S(1)} %get-tuple-element.51.refs_0_.refs_1_, bf16[1,3,768,384]{3,2,1,0:T(8,128)(2,1)S(1)} %get-tuple-element.49.refs_4_.refs_1_.refs_0_.refs_2_, bf16[1,384,768]{2,1,0:T(8,128)(2,1)S(1)} %get-tuple-element.50.refs_5_.refs_2_.refs_1_, ...), custom_call_target="tpu_custom_call" | custom-call | flops 150994944 | bytes 2752512 | tf_op jit(solution)/shard_map/fore/pallas_call | solution.py:421
  13.4 0.8 %collective-permute-start.4 = (bf16[64,768]{1,0:T(8,128)(2,1)S(1)}, bf16[64,768]{1,0:T(8,128)(2,1)S(1)}, u32[]{:S(2)}, u32[]{:S(2)}) collective-permute-start(bf16[64,768]{1,0:T(8,128)(2,1)S(1)} %get-tuple-element.53.refs_4_), channel_id=1, source_target_pairs={{0,4},{1,5},{2,6},{3,7},{4,0},{5,1},{6,2},{7,3},{8,24},{9,25},{10,... | collective-permute-start | bytes 294920 | tf_op jit(solution)/shard_map/ppermute | solution.py:467
  14.3 2.9 %collective-permute-done.3.refs_0_.refs_2_.refs_1_ = bf16[64,768]{1,0:T(8,128)(2,1)S(1)} collective-permute-done((bf16[64,768]{1,0:T(8,128)(2,1)S(1)}, bf16[64,768]{1,0:T(8,128)(2,1)S(1)}, u32[]{:S(2)}, u32[]{:S(2)}) %collective-permute-start.3) | collective-permute-done | bytes 98336 | tf_op jit(solution)/shard_map/ppermute | solution.py:467
  17.2 2.1 %collective-permute-done.4.refs_0_.refs_3_.refs_2_ = bf16[64,768]{1,0:T(8,128)(2,1)S(1)} collective-permute-done((bf16[64,768]{1,0:T(8,128)(2,1)S(1)}, bf16[64,768]{1,0:T(8,128)(2,1)S(1)}, u32[]{:S(2)}, u32[]{:S(2)}) %collective-permute-start.4) | collective-permute-done | bytes 98336 | tf_op jit(solution)/shard_map/ppermute | solution.py:467
  19.3 0.7 %transpose.1 = (bf16[1,3,384,768]{3,2,1,0:T(8,128)(2,1)S(1)}, bf16[1,768,384]{2,1,0:T(8,128)(2,1)S(1)}) custom-call(bf16[1,3,768,384]{3,2,1,0:T(8,128)(2,1)S(1)} %get-tuple-element.49.refs_4_.refs_1_.refs_0_.refs_2_, bf16[1,384,768]{2,1,0:T(8,128)(2,1)S(1)} %get-tuple-element.50.refs_5_.refs_2_.refs_1_, ...), custom_call_target="tpu_custom_call" | custom-call | bytes 4718592 | tf_op jit(solution)/shard_map/transpose/pallas_call | solution.py:421
  20.0 3.2 %collective-permute-start.7 = (bf16[64,768]{1,0:T(8,128)(2,1)S(1)}, bf16[64,768]{1,0:T(8,128)(2,1)S(1)}, u32[]{:S(2)}, u32[]{:S(2)}) collective-permute-start(bf16[64,768]{1,0:T(8,128)(2,1)S(1)} %get-tuple-element.58.refs_3_.refs_12_.refs_5_), channel_id=1, source_target_pairs={{0,8},{1,9},{2,10},{3,11},{4,20},{5,21},{6,22},{7,23},{8,12},{9,13... | collective-permute-start | bytes 294920 | tf_op jit(solution)/shard_map/ppermute | solution.py:467
  23.2 1.1 %collective-permute-start.8 = (bf16[64,768]{1,0:T(8,128)(2,1)S(1)}, bf16[64,768]{1,0:T(8,128)(2,1)S(1)}, u32[]{:S(2)}, u32[]{:S(2)}) collective-permute-start(bf16[64,768]{1,0:T(8,128)(2,1)S(1)} %get-tuple-element.59.refs_13_.refs_6_), channel_id=1, source_target_pairs={{0,8},{1,9},{2,10},{3,11},{4,20},{5,21},{6,22},{7,23},{8,12},{9,13... | collective-permute-start | bytes 294920 | tf_op jit(solution)/shard_map/ppermute | solution.py:467
  24.6 1.9 %collective-permute-done.7.refs_0_.refs_5_ = bf16[64,768]{1,0:T(8,128)(2,1)S(1)} collective-permute-done((bf16[64,768]{1,0:T(8,128)(2,1)S(1)}, bf16[64,768]{1,0:T(8,128)(2,1)S(1)}, u32[]{:S(2)}, u32[]{:S(2)}) %collective-permute-start.7) | collective-permute-done | bytes 98336 | tf_op jit(solution)/shard_map/ppermute | solution.py:467
  26.5 2.9 %collective-permute-done.8.refs_0_.refs_6_ = bf16[64,768]{1,0:T(8,128)(2,1)S(1)} collective-permute-done((bf16[64,768]{1,0:T(8,128)(2,1)S(1)}, bf16[64,768]{1,0:T(8,128)(2,1)S(1)}, u32[]{:S(2)}, u32[]{:S(2)}) %collective-permute-start.8) | collective-permute-done | bytes 98336 | tf_op jit(solution)/shard_map/ppermute | solution.py:467
  29.5 0.6 columns.1
  30.4 2.8 %collective-permute-start.14 = (bf16[64,768]{1,0:T(8,128)(2,1)S(1)}, bf16[64,768]{1,0:T(8,128)(2,1)S(1)}, u32[]{:S(2)}, u32[]{:S(2)}) collective-permute-start(bf16[64,768]{1,0:T(8,128)(2,1)S(1)} %get-tuple-element.75.refs_5_.refs_2_), channel_id=1, source_target_pairs={{0,8},{1,9},{2,10},{3,11},{4,0},{5,1},{6,2},{7,3},{8,4},{9,5},{10,... | collective-permute-start | bytes 294920 | tf_op jit(solution)/shard_map/ppermute | solution.py:467
  33.2 2.1 %collective-permute-done.9.refs_1_.refs_2_ = bf16[384,128]{1,0:T(8,128)(2,1)S(1)} collective-permute-done((bf16[384,128]{1,0:T(8,128)(2,1)S(1)}, bf16[384,128]{1,0:T(8,128)(2,1)S(1)}, u32[]{:S(2)}, u32[]{:S(2)}) %collective-permute-start.9) | collective-permute-done | bytes 98336 | tf_op jit(solution)/shard_map/ppermute | solution.py:473
  35.3 1.4 %collective-permute-start.12 = (bf16[384,128]{1,0:T(8,128)(2,1)S(1)}, bf16[384,128]{1,0:T(8,128)(2,1)S(1)}, u32[]{:S(2)}, u32[]{:S(2)}) collective-permute-start(bf16[384,128]{1,0:T(8,128)(2,1)S(1)} %message.1.refs_7_), channel_id=1, source_target_pairs={{0,2},{1,3},{2,0},{3,1},{4,6},{5,7},{6,4},{7,5},{8,10},{9,11},{10,... | collective-permute-start | bytes 294920 | tf_op jit(solution)/shard_map/ppermute | solution.py:473
  36.8 0.7 %collective-permute-start.16 = (bf16[64,768]{1,0:T(8,128)(2,1)S(1)}, bf16[64,768]{1,0:T(8,128)(2,1)S(1)}, u32[]{:S(2)}, u32[]{:S(2)}) collective-permute-start(bf16[64,768]{1,0:T(8,128)(2,1)S(1)} %get-tuple-element.77.refs_5_.refs_6_), channel_id=1, source_target_pairs={{0,12},{1,13},{2,14},{3,15},{4,0},{5,1},{6,2},{7,3},{8,24},{9,25},... | collective-permute-start | bytes 294920 | tf_op jit(solution)/shard_map/ppermute | solution.py:467
  37.5 2.7 %collective-permute-start.15 = (bf16[64,768]{1,0:T(8,128)(2,1)S(1)}, bf16[64,768]{1,0:T(8,128)(2,1)S(1)}, u32[]{:S(2)}, u32[]{:S(2)}) collective-permute-start(bf16[64,768]{1,0:T(8,128)(2,1)S(1)} %get-tuple-element.78.refs_7_), channel_id=1, source_target_pairs={{0,12},{1,13},{2,14},{3,15},{4,0},{5,1},{6,2},{7,3},{8,24},{9,25},... | collective-permute-start | bytes 294920 | tf_op jit(solution)/shard_map/ppermute | solution.py:467
  40.2 2.5 %collective-permute-done.12.refs_8_.refs_1_.refs_3_ = bf16[384,128]{1,0:T(8,128)(2,1)S(1)} collective-permute-done((bf16[384,128]{1,0:T(8,128)(2,1)S(1)}, bf16[384,128]{1,0:T(8,128)(2,1)S(1)}, u32[]{:S(2)}, u32[]{:S(2)}) %collective-permute-start.12) | collective-permute-done | bytes 98336 | tf_op jit(solution)/shard_map/ppermute | solution.py:473
  43.4 2.5 %collective-permute-start.17 = (bf16[128,384]{1,0:T(8,128)(2,1)S(1)}, bf16[128,384]{1,0:T(8,128)(2,1)S(1)}, u32[]{:S(2)}, u32[]{:S(2)}) collective-permute-start(bf16[128,384]{1,0:T(8,128)(2,1)S(1)} %head.3.refs_4_), channel_id=1, source_target_pairs={{0,2},{1,3},{2,0},{3,1},{4,6},{5,7},{6,4},{7,5},{8,10},{9,11},{10,... | collective-permute-start | bytes 294920 | tf_op jit(solution)/shard_map/ppermute | solution.py:473
  45.9 0.6 collective-permute-start.18
  46.5 4.6 %collective-permute-done.17.refs_5_ = bf16[128,384]{1,0:T(8,128)(2,1)S(1)} collective-permute-done((bf16[128,384]{1,0:T(8,128)(2,1)S(1)}, bf16[128,384]{1,0:T(8,128)(2,1)S(1)}, u32[]{:S(2)}, u32[]{:S(2)}) %collective-permute-start.17) | collective-permute-done | bytes 98336 | tf_op jit(solution)/shard_map/ppermute | solution.py:473
  51.4 4.3 %collective-permute-done.19.refs_7_ = bf16[128,384]{1,0:T(8,128)(2,1)S(1)} collective-permute-done((bf16[128,384]{1,0:T(8,128)(2,1)S(1)}, bf16[128,384]{1,0:T(8,128)(2,1)S(1)}, u32[]{:S(2)}, u32[]{:S(2)}) %collective-permute-start.19) | collective-permute-done | bytes 98336 | tf_op jit(solution)/shard_map/ppermute | solution.py:473
  56.5 1.1 %collective-permute-done.20 = bf16[3,96,384]{2,1,0:T(8,128)(2,1)S(1)} collective-permute-done((bf16[3,96,384]{2,1,0:T(8,128)(2,1)S(1)}, bf16[3,96,384]{2,1,0:T(8,128)(2,1)S(1)}, u32[]{:S(2)}, u32[]{:S(2)}) %collective-permute-start.20) | collective-permute-done | bytes 221216 | tf_op jit(solution)/shard_map/ppermute | solution.py:636
  57.6 0.8 %add_bitcast_fusion = f32[1,3,96,384]{3,2,1,0:T(8,128)} fusion(f32[3,96,384]{2,1,0:T(8,128)S(1)} %grad.3, bf16[3,96,384]{2,1,0:T(8,128)(2,1)S(1)} %collective-permute-done.20), kind=kLoop, calls=%fused_computation | loop fusion | flops 221184 | bytes 1105920 | tf_op jit(solution)/shard_map/broadcast_in_dim | solution.py:637
  (38 shorter events, 2.7 us)
Async XLA Ops:
  1.0 6.4 %copy-start = (bf16[1,3,768,384]{3,2,1,0:T(8,128)(2,1)S(1)}, bf16[1,3,768,384]{3,2,1,0:T(8,128)(2,1)}, u32[]{:S(2)}) copy-start(bf16[1,3,768,384]{3,2,1,0:T(8,128)(2,1)} %refs_0_.1) | copy-start | bytes 5308420
  1.0 6.4 %copy-start.1 = (bf16[1,384,768]{2,1,0:T(8,128)(2,1)S(1)}, bf16[1,384,768]{2,1,0:T(8,128)(2,1)}, u32[]{:S(2)}) copy-start(bf16[1,384,768]{2,1,0:T(8,128)(2,1)} %refs_1_.1) | copy-start | bytes 1769476
  1.2 7.3 %collective-permute-start = (bf16[32,768]{1,0:T(8,128)(2,1)S(1)}, bf16[32,768]{1,0:T(8,128)(2,1)S(1)}, u32[]{:S(2)}, u32[]{:S(2)}) collective-permute-start(bf16[32,768]{1,0:T(8,128)(2,1)S(1)} %get-tuple-element.45), channel_id=1, source_target_pairs={{0,1},{1,2},{2,3},{3,0},{4,5},{5,6},{6,7},{7,4},{8,9},{9,10},{10,1... | collective-permute-start | bytes 147464 | tf_op jit(solution)/shard_map/ppermute | solution.py:470
  4.3 4.6 %collective-permute-start.1 = (bf16[32,768]{1,0:T(8,128)(2,1)S(1)}, bf16[32,768]{1,0:T(8,128)(2,1)S(1)}, u32[]{:S(2)}, u32[]{:S(2)}) collective-permute-start(bf16[32,768]{1,0:T(8,128)(2,1)S(1)} %get-tuple-element.46), channel_id=1, source_target_pairs={{0,3},{1,0},{2,1},{3,2},{4,7},{5,4},{6,5},{7,6},{8,11},{9,8},{10,9... | collective-permute-start | bytes 147464 | tf_op jit(solution)/shard_map/ppermute | solution.py:470
  6.4 5.1 %collective-permute-start.2 = (bf16[32,768]{1,0:T(8,128)(2,1)S(1)}, bf16[32,768]{1,0:T(8,128)(2,1)S(1)}, u32[]{:S(2)}, u32[]{:S(2)}) collective-permute-start(bf16[32,768]{1,0:T(8,128)(2,1)S(1)} %get-tuple-element.47), channel_id=1, source_target_pairs={{0,2},{1,3},{2,0},{3,1},{4,6},{5,7},{6,4},{7,5},{8,10},{9,11},{10,... | collective-permute-start | bytes 147464 | tf_op jit(solution)/shard_map/ppermute | solution.py:470
  12.2 5.0 %collective-permute-start.3 = (bf16[64,768]{1,0:T(8,128)(2,1)S(1)}, bf16[64,768]{1,0:T(8,128)(2,1)S(1)}, u32[]{:S(2)}, u32[]{:S(2)}) collective-permute-start(bf16[64,768]{1,0:T(8,128)(2,1)S(1)} %get-tuple-element.52.refs_3_), channel_id=1, source_target_pairs={{0,4},{1,5},{2,6},{3,7},{4,0},{5,1},{6,2},{7,3},{8,24},{9,25},{10,... | collective-permute-start | bytes 294920 | tf_op jit(solution)/shard_map/ppermute | solution.py:467
  13.4 5.8 %collective-permute-start.4 = (bf16[64,768]{1,0:T(8,128)(2,1)S(1)}, bf16[64,768]{1,0:T(8,128)(2,1)S(1)}, u32[]{:S(2)}, u32[]{:S(2)}) collective-permute-start(bf16[64,768]{1,0:T(8,128)(2,1)S(1)} %get-tuple-element.53.refs_4_), channel_id=1, source_target_pairs={{0,4},{1,5},{2,6},{3,7},{4,0},{5,1},{6,2},{7,3},{8,24},{9,25},{10,... | collective-permute-start | bytes 294920 | tf_op jit(solution)/shard_map/ppermute | solution.py:467
  17.1 2.8 %collective-permute-start.5 = (bf16[64,768]{1,0:T(8,128)(2,1)S(1)}, bf16[64,768]{1,0:T(8,128)(2,1)S(1)}, u32[]{:S(2)}, u32[]{:S(2)}) collective-permute-start(bf16[64,768]{1,0:T(8,128)(2,1)S(1)} %get-tuple-element.54.refs_3_.refs_2_), channel_id=1, source_target_pairs={{0,16},{1,17},{2,18},{3,19},{4,8},{5,9},{6,10},{7,11},{8,12},{9,13... | collective-permute-start | bytes 294920 | tf_op jit(solution)/shard_map/ppermute | solution.py:467
  19.3 3.9 %collective-permute-start.6 = (bf16[64,768]{1,0:T(8,128)(2,1)S(1)}, bf16[64,768]{1,0:T(8,128)(2,1)S(1)}, u32[]{:S(2)}, u32[]{:S(2)}) collective-permute-start(bf16[64,768]{1,0:T(8,128)(2,1)S(1)} %get-tuple-element.55.refs_3_.refs_4_), channel_id=1, source_target_pairs={{0,16},{1,17},{2,18},{3,19},{4,8},{5,9},{6,10},{7,11},{8,4},{9,5},... | collective-permute-start | bytes 294920 | tf_op jit(solution)/shard_map/ppermute | solution.py:467
  20.0 6.5 %collective-permute-start.7 = (bf16[64,768]{1,0:T(8,128)(2,1)S(1)}, bf16[64,768]{1,0:T(8,128)(2,1)S(1)}, u32[]{:S(2)}, u32[]{:S(2)}) collective-permute-start(bf16[64,768]{1,0:T(8,128)(2,1)S(1)} %get-tuple-element.58.refs_3_.refs_12_.refs_5_), channel_id=1, source_target_pairs={{0,8},{1,9},{2,10},{3,11},{4,20},{5,21},{6,22},{7,23},{8,12},{9,13... | collective-permute-start | bytes 294920 | tf_op jit(solution)/shard_map/ppermute | solution.py:467
  23.2 6.3 %collective-permute-start.8 = (bf16[64,768]{1,0:T(8,128)(2,1)S(1)}, bf16[64,768]{1,0:T(8,128)(2,1)S(1)}, u32[]{:S(2)}, u32[]{:S(2)}) collective-permute-start(bf16[64,768]{1,0:T(8,128)(2,1)S(1)} %get-tuple-element.59.refs_13_.refs_6_), channel_id=1, source_target_pairs={{0,8},{1,9},{2,10},{3,11},{4,20},{5,21},{6,22},{7,23},{8,12},{9,13... | collective-permute-start | bytes 294920 | tf_op jit(solution)/shard_map/ppermute | solution.py:467
  26.5 3.9 %collective-permute-start.10 = (bf16[64,768]{1,0:T(8,128)(2,1)S(1)}, bf16[64,768]{1,0:T(8,128)(2,1)S(1)}, u32[]{:S(2)}, u32[]{:S(2)}) collective-permute-start(bf16[64,768]{1,0:T(8,128)(2,1)S(1)} %get-tuple-element.70.refs_5_.refs_7_), channel_id=1, source_target_pairs={{0,16},{1,17},{2,18},{3,19},{4,20},{5,21},{6,22},{7,23},{8,12},{9,... | collective-permute-start | bytes 294920 | tf_op jit(solution)/shard_map/ppermute | solution.py:467
  29.5 3.7 %collective-permute-start.11 = (bf16[64,768]{1,0:T(8,128)(2,1)S(1)}, bf16[64,768]{1,0:T(8,128)(2,1)S(1)}, u32[]{:S(2)}, u32[]{:S(2)}) collective-permute-start(bf16[64,768]{1,0:T(8,128)(2,1)S(1)} %get-tuple-element.71.refs_8_), channel_id=1, source_target_pairs={{0,16},{1,17},{2,18},{3,19},{4,20},{5,21},{6,22},{7,23},{8,12},{9,... | collective-permute-start | bytes 294920 | tf_op jit(solution)/shard_map/ppermute | solution.py:467
  30.0 5.3 %collective-permute-start.9 = (bf16[384,128]{1,0:T(8,128)(2,1)S(1)}, bf16[384,128]{1,0:T(8,128)(2,1)S(1)}, u32[]{:S(2)}, u32[]{:S(2)}) collective-permute-start(bf16[384,128]{1,0:T(8,128)(2,1)S(1)} %get-tuple-element.74), channel_id=1, source_target_pairs={{0,1},{1,0},{2,3},{3,2},{4,5},{5,4},{6,7},{7,6},{8,9},{9,8},{10,11... | collective-permute-start | bytes 294920 | tf_op jit(solution)/shard_map/ppermute | solution.py:473
  30.4 6.4 %collective-permute-start.14 = (bf16[64,768]{1,0:T(8,128)(2,1)S(1)}, bf16[64,768]{1,0:T(8,128)(2,1)S(1)}, u32[]{:S(2)}, u32[]{:S(2)}) collective-permute-start(bf16[64,768]{1,0:T(8,128)(2,1)S(1)} %get-tuple-element.75.refs_5_.refs_2_), channel_id=1, source_target_pairs={{0,8},{1,9},{2,10},{3,11},{4,0},{5,1},{6,2},{7,3},{8,4},{9,5},{10,... | collective-permute-start | bytes 294920 | tf_op jit(solution)/shard_map/ppermute | solution.py:467
  33.2 4.3 %collective-permute-start.13 = (bf16[64,768]{1,0:T(8,128)(2,1)S(1)}, bf16[64,768]{1,0:T(8,128)(2,1)S(1)}, u32[]{:S(2)}, u32[]{:S(2)}) collective-permute-start(bf16[64,768]{1,0:T(8,128)(2,1)S(1)} %get-tuple-element.76.refs_3_.refs_6_), channel_id=1, source_target_pairs={{0,16},{1,17},{2,18},{3,19},{4,8},{5,9},{6,10},{7,11},{8,4},{9,5},... | collective-permute-start | bytes 294920 | tf_op jit(solution)/shard_map/ppermute | solution.py:467
  35.3 7.4 %collective-permute-start.12 = (bf16[384,128]{1,0:T(8,128)(2,1)S(1)}, bf16[384,128]{1,0:T(8,128)(2,1)S(1)}, u32[]{:S(2)}, u32[]{:S(2)}) collective-permute-start(bf16[384,128]{1,0:T(8,128)(2,1)S(1)} %message.1.refs_7_), channel_id=1, source_target_pairs={{0,2},{1,3},{2,0},{3,1},{4,6},{5,7},{6,4},{7,5},{8,10},{9,11},{10,... | collective-permute-start | bytes 294920 | tf_op jit(solution)/shard_map/ppermute | solution.py:473
  36.8 6.0 %collective-permute-start.16 = (bf16[64,768]{1,0:T(8,128)(2,1)S(1)}, bf16[64,768]{1,0:T(8,128)(2,1)S(1)}, u32[]{:S(2)}, u32[]{:S(2)}) collective-permute-start(bf16[64,768]{1,0:T(8,128)(2,1)S(1)} %get-tuple-element.77.refs_5_.refs_6_), channel_id=1, source_target_pairs={{0,12},{1,13},{2,14},{3,15},{4,0},{5,1},{6,2},{7,3},{8,24},{9,25},... | collective-permute-start | bytes 294920 | tf_op jit(solution)/shard_map/ppermute | solution.py:467
  37.5 5.7 %collective-permute-start.15 = (bf16[64,768]{1,0:T(8,128)(2,1)S(1)}, bf16[64,768]{1,0:T(8,128)(2,1)S(1)}, u32[]{:S(2)}, u32[]{:S(2)}) collective-permute-start(bf16[64,768]{1,0:T(8,128)(2,1)S(1)} %get-tuple-element.78.refs_7_), channel_id=1, source_target_pairs={{0,12},{1,13},{2,14},{3,15},{4,0},{5,1},{6,2},{7,3},{8,24},{9,25},... | collective-permute-start | bytes 294920 | tf_op jit(solution)/shard_map/ppermute | solution.py:467
  43.4 7.6 %collective-permute-start.17 = (bf16[128,384]{1,0:T(8,128)(2,1)S(1)}, bf16[128,384]{1,0:T(8,128)(2,1)S(1)}, u32[]{:S(2)}, u32[]{:S(2)}) collective-permute-start(bf16[128,384]{1,0:T(8,128)(2,1)S(1)} %head.3.refs_4_), channel_id=1, source_target_pairs={{0,2},{1,3},{2,0},{3,1},{4,6},{5,7},{6,4},{7,5},{8,10},{9,11},{10,... | collective-permute-start | bytes 294920 | tf_op jit(solution)/shard_map/ppermute | solution.py:473
  45.9 5.4 %collective-permute-start.18 = (bf16[128,384]{1,0:T(8,128)(2,1)S(1)}, bf16[128,384]{1,0:T(8,128)(2,1)S(1)}, u32[]{:S(2)}, u32[]{:S(2)}) collective-permute-start(bf16[128,384]{1,0:T(8,128)(2,1)S(1)} %head.3.refs_4_), channel_id=1, source_target_pairs={{0,1},{1,0},{2,3},{3,2},{4,5},{5,4},{6,7},{7,6},{8,9},{9,8},{10,11... | collective-permute-start | bytes 294920 | tf_op jit(solution)/shard_map/ppermute | solution.py:473
  51.0 4.6 %collective-permute-start.19 = (bf16[128,384]{1,0:T(8,128)(2,1)S(1)}, bf16[128,384]{1,0:T(8,128)(2,1)S(1)}, u32[]{:S(2)}, u32[]{:S(2)}) collective-permute-start(bf16[128,384]{1,0:T(8,128)(2,1)S(1)} %collective-permute-done.17.refs_5_), channel_id=1, source_target_pairs={{0,1},{1,0},{2,3},{3,2},{4,5},{5,4},{6,7},{7,6},{8,9},{9,8},{10,11... | collective-permute-start | bytes 294920 | tf_op jit(solution)/shard_map/ppermute | solution.py:473
  56.1 1.5 %collective-permute-start.20 = (bf16[3,96,384]{2,1,0:T(8,128)(2,1)S(1)}, bf16[3,96,384]{2,1,0:T(8,128)(2,1)S(1)}, u32[]{:S(2)}, u32[]{:S(2)}) collective-permute-start(bf16[3,96,384]{2,1,0:T(8,128)(2,1)S(1)} %grad.2.refs_8_), channel_id=1, source_target_pairs={{0,16},{16,0},{1,17},{17,1},{2,18},{18,2},{3,19},{19,3},{4,20},{20... | collective-permute-start | bytes 663560 | tf_op jit(solution)/shard_map/ppermute | solution.py:636
